TPU v7x, 32 devices: a whole 2x2x4 slice. The times are simulated.
32 devices in a mesh: ctx: 16 (over z, x, core), tp: 2 (over y).
Axes of the slice: x: 2, y: 2, z: 4, core: 2. Of those that a mesh axis runs over, the one named last changes fastest.
Arguments:
- states: bfloat16 [4096, 1024], P('ctx'), may hold values from -6 to 6
- span_order: int32 [16, 4], P('ctx'), may hold values from 0 to 31, as said below
- attn_gain: bfloat16 [1024], P('ctx'), may hold values from 0.5 to 1.5
- w_query: bfloat16 [1024, 1024], P('ctx', 'tp'), may hold values from -0.1875 to 0.1875
- w_key: bfloat16 [1024, 512], P('ctx', 'tp'), may hold values from -0.1875 to 0.1875
- w_value: bfloat16 [1024, 512], P('ctx', 'tp'), may hold values from -0.1875 to 0.1875
- query_gain: bfloat16 [64], P('ctx'), may hold values from 0.5 to 1.5
- key_gain: bfloat16 [64], P('ctx'), may hold values from 0.5 to 1.5
- w_out: bfloat16 [1024, 1024], P('tp', 'ctx'), may hold values from -1.5 to 1.5
- ffn_gain: bfloat16 [1024], P('ctx'), may hold values from 0.5 to 1.5
- w_gate: bfloat16 [1024, 4608], P('ctx', 'tp'), may hold values from -0.1875 to 0.1875
- w_up: bfloat16 [1024, 4608], P('ctx', 'tp'), may hold values from -0.1875 to 0.1875
- w_down: bfloat16 [4608, 1024], P('tp', 'ctx'), may hold values from -0.09375 to 0.09375
- grad_out: bfloat16 [4096, 1024], P('ctx'), may hold values from -6 to 6
Outputs:
- output: bfloat16 [4096, 1024], P('ctx')
- grad_states: float32 [4096, 1024], P('ctx')
- grad_attn_gain: float32 [1024], P('ctx')
- grad_query: float32 [1024, 1024], P('ctx', 'tp')
- grad_key: float32 [1024, 512], P('ctx', 'tp')
- grad_value: float32 [1024, 512], P('ctx', 'tp')
- grad_query_gain: float32 [64], P('ctx')
- grad_key_gain: float32 [64], P('ctx')
- grad_proj: float32 [1024, 1024], P('tp', 'ctx')
- grad_ffn_gain: float32 [1024], P('ctx')
- grad_gate: float32 [1024, 4608], P('ctx', 'tp')
- grad_up: float32 [1024, 4608], P('ctx', 'tp')
- grad_down: float32 [4608, 1024], P('tp', 'ctx')
Inputs may be any that keep to these rules, and one draw needn't show every extreme that they name: `span_order`: in each row c the two columns 2 s and 2 s + 1 hold p and 31 - p for some p; every span of every sequence is held exactly once.
All inputs are finite; a program needn't handle non-finite values.
Results may differ from a plain program's by a relative error of at most 0.03.
Values may be sent and summed in bfloat16 or wider, within the bound.
A program may use at most 128 MiB of HBM per device.

v0:
```python
import math

import jax
import jax.numpy as jnp
from jax import lax
from jax.sharding import PartitionSpec as P

DH = 64


EPS = 1e-05
THETA = 1000000.0
SCALE = 0.125


def passed_along(shard, axis, by):
    devices = lax.axis_size(axis)
    return lax.ppermute(shard, axis, [(i, (i + by) % devices) for i in range(devices)])


def product(left, right):
    return jnp.dot(left, right, preferred_element_type=jnp.float32)


def norm_rows(values):
    factor = lax.rsqrt(jnp.mean(values * values, axis=-1, keepdims=True) + EPS)
    return (values * factor, factor)


def norm_back(gradient, normed, factor, gain):
    scaled = gradient * gain
    return factor * (scaled - normed * jnp.mean(scaled * normed, axis=-1, keepdims=True))


def rotate(values, cosine, sine_part):
    half_dim = values.shape[-1] // 2
    first_half = values[..., :half_dim]
    second_half = values[..., half_dim:]
    return jnp.concatenate(
        [
            first_half * cosine - second_half * sine_part,
            second_half * cosine + first_half * sine_part,
        ],
        axis=-1,
    )


def to_heads(flattened, sequences, key_heads, group_size):
    row_count = flattened.size // (sequences * key_heads * group_size * DH)
    arranged = flattened.reshape(sequences, row_count, key_heads, group_size, DH)
    return arranged.transpose(0, 2, 3, 1, 4).reshape(
        sequences, key_heads, group_size * row_count, DH
    )


def from_heads(stacked, group_size):
    sequences = stacked.shape[0]
    key_heads = stacked.shape[1]
    row_count = stacked.shape[2] // group_size
    arranged = stacked.reshape(sequences, key_heads, group_size, row_count, DH).transpose(
        0, 3, 1, 2, 4
    )
    return arranged.reshape(sequences * row_count, key_heads * group_size * DH)


def shards(
    states,
    span_order,
    attn_gain,
    w_query,
    w_key,
    w_value,
    query_gain,
    key_gain,
    w_out,
    ffn_gain,
    w_gate,
    w_up,
    w_down,
    grad_out,
):
    ctx_count = lax.axis_size("ctx")
    own_index = lax.axis_index("ctx")
    token_rows = states.shape[0]
    sequences = span_order.shape[1] // 2
    seq_rows = token_rows // sequences
    span_len = seq_rows // 2
    order_table = lax.all_gather(span_order, "ctx", axis=0, tiled=True)
    offsets = jnp.arange(span_len, dtype=jnp.int32)
    every_place = (order_table.reshape(ctx_count, sequences, 2, 1) * span_len + offsets).reshape(
        ctx_count, sequences, seq_rows
    )
    own_place = lax.dynamic_index_in_dim(every_place, own_index, 0, keepdims=False)
    flat_place = jnp.transpose(every_place, (1, 0, 2)).reshape(sequences, ctx_count * seq_rows)
    gathered = (
        lax.all_gather(attn_gain, "ctx", axis=0, tiled=True),
        lax.all_gather(w_query, "ctx", axis=0, tiled=True),
        lax.all_gather(w_key, "ctx", axis=0, tiled=True),
        lax.all_gather(w_value, "ctx", axis=0, tiled=True),
        lax.all_gather(query_gain, "ctx", axis=0, tiled=True),
        lax.all_gather(key_gain, "ctx", axis=0, tiled=True),
        lax.all_gather(w_out, "ctx", axis=1, tiled=True),
        lax.all_gather(ffn_gain, "ctx", axis=0, tiled=True),
        lax.all_gather(w_gate, "ctx", axis=0, tiled=True),
        lax.all_gather(w_up, "ctx", axis=0, tiled=True),
        lax.all_gather(w_down, "ctx", axis=1, tiled=True),
    )
    (
        gain_attn,
        query_full,
        key_full,
        value_full,
        gain_query,
        gain_key,
        out_full,
        gain_ffn,
        gate_full,
        up_full,
        down_full,
    ) = gathered
    query_heads = query_full.shape[1] // DH
    key_heads = key_full.shape[1] // DH
    group_size = query_heads // key_heads
    query_rows = group_size * seq_rows
    inputs = states.astype(jnp.float32)
    normed_one, factor_one = norm_rows(inputs)
    hidden_one = (normed_one * gain_attn.astype(jnp.float32)).astype(jnp.bfloat16)
    query_pre = product(hidden_one, query_full).reshape(token_rows, query_heads, DH)
    key_pre = product(hidden_one, key_full).reshape(token_rows, key_heads, DH)
    value_low = product(hidden_one, value_full).astype(jnp.bfloat16)
    half_dim = DH // 2
    inverse_freq = jnp.exp(-math.log(THETA) * jnp.arange(half_dim, dtype=jnp.float32) / half_dim)
    angles = own_place.reshape(token_rows).astype(jnp.float32)[:, None] * inverse_freq[None, :]
    cosine = jnp.cos(angles)[:, None, :]
    sine_part = jnp.sin(angles)[:, None, :]
    query_normed, query_factor = norm_rows(query_pre)
    key_normed, key_factor = norm_rows(key_pre)
    query_rot = rotate(query_normed * gain_query.astype(jnp.float32), cosine, sine_part).astype(
        jnp.bfloat16
    )
    key_rot = rotate(key_normed * gain_key.astype(jnp.float32), cosine, sine_part).astype(
        jnp.bfloat16
    )
    queries = to_heads(query_rot, sequences, key_heads, group_size)
    keys = to_heads(key_rot, sequences, key_heads, 1)
    values = to_heads(value_low, sequences, key_heads, 1)
    query_place = jnp.tile(own_place, (1, group_size))

    def scores_for(key_block, place_block):
        raw_scores = (
            jnp.einsum("shrd,shkd->shrk", queries, key_block, preferred_element_type=jnp.float32)
            * SCALE
        )
        visible = place_block[:, None, None, :] <= query_place[:, None, :, None]
        return jnp.where(visible, raw_scores, -jnp.inf)

    start_state = (
        jnp.full((sequences, key_heads, query_rows), -1e30, jnp.float32),
        jnp.zeros((sequences, key_heads, query_rows), jnp.float32),
        jnp.zeros((sequences, key_heads, query_rows, DH), jnp.float32),
    )
    running = start_state
    key_piece = lax.all_gather(keys, "ctx", axis=2, tiled=True)
    value_piece = lax.all_gather(values, "ctx", axis=2, tiled=True)
    row_count = key_piece.shape[2]
    block_rows = math.gcd(row_count, seq_rows)
    block_count = row_count // block_rows
    key_blocks = jnp.moveaxis(
        key_piece.reshape(sequences, key_heads, block_count, block_rows, DH), 2, 0
    )
    value_blocks = jnp.moveaxis(
        value_piece.reshape(sequences, key_heads, block_count, block_rows, DH), 2, 0
    )
    place_blocks = jnp.moveaxis(flat_place.reshape(sequences, block_count, block_rows), 1, 0)

    def block_step(state_now, blocks):
        running_max, row_total, weighted = state_now
        key_block, value_block, place_block = blocks
        scores = scores_for(key_block, place_block)
        new_max = jnp.maximum(running_max, jnp.max(scores, axis=-1))
        shrink = jnp.exp(running_max - new_max)
        weights = jnp.exp(scores - new_max[..., None])
        row_total = row_total * shrink + jnp.sum(weights, axis=-1)
        weighted = weighted * shrink[..., None] + jnp.einsum(
            "shrk,shkd->shrd",
            weights.astype(jnp.bfloat16),
            value_block,
            preferred_element_type=jnp.float32,
        )
        return ((new_max, row_total, weighted), None)

    running, unused = lax.scan(block_step, running, (key_blocks, value_blocks, place_blocks))
    running_max, row_total, weighted = running
    attended = weighted / row_total[..., None]
    log_total = running_max + jnp.log(row_total)
    mixed_low = from_heads(attended, group_size).astype(jnp.bfloat16)
    attn_terms = product(mixed_low, out_full)
    attn_branch = lax.psum(attn_terms.astype(jnp.bfloat16), "tp").astype(jnp.float32)
    middle = inputs + attn_branch
    normed_two, factor_two = norm_rows(middle)
    hidden_two = (normed_two * gain_ffn.astype(jnp.float32)).astype(jnp.bfloat16)
    gate_proj = product(hidden_two, gate_full)
    up_proj = product(hidden_two, up_full)
    sigmoid_gate = 1.0 / (1.0 + jnp.exp(-gate_proj))
    activated = gate_proj * sigmoid_gate
    inner = (activated * up_proj).astype(jnp.bfloat16)
    ffn_terms = product(inner, down_full)
    ffn_branch = lax.psum(ffn_terms.astype(jnp.bfloat16), "tp").astype(jnp.float32)
    output_low = (middle + ffn_branch).astype(jnp.bfloat16)
    weights_back = (
        lax.all_gather(attn_gain, "ctx", axis=0, tiled=True),
        lax.all_gather(w_query, "ctx", axis=0, tiled=True),
        lax.all_gather(w_key, "ctx", axis=0, tiled=True),
        lax.all_gather(w_value, "ctx", axis=0, tiled=True),
        lax.all_gather(query_gain, "ctx", axis=0, tiled=True),
        lax.all_gather(key_gain, "ctx", axis=0, tiled=True),
        lax.all_gather(w_out, "ctx", axis=1, tiled=True),
        lax.all_gather(ffn_gain, "ctx", axis=0, tiled=True),
        lax.all_gather(w_gate, "ctx", axis=0, tiled=True),
        lax.all_gather(w_up, "ctx", axis=0, tiled=True),
        lax.all_gather(w_down, "ctx", axis=1, tiled=True),
    )
    (
        gain_attn_back,
        query_back,
        key_back,
        value_back,
        gain_query_back,
        gain_key_back,
        out_back,
        gain_ffn_back,
        gate_back,
        up_back,
        down_back,
    ) = weights_back
    down_grad = jnp.einsum("tf,td->fd", inner, grad_out, preferred_element_type=jnp.float32)
    inner_grad = jnp.einsum("td,fd->tf", grad_out, down_back, preferred_element_type=jnp.float32)
    gate_grad = (
        inner_grad * up_proj * sigmoid_gate * (1.0 + gate_proj * (1.0 - sigmoid_gate))
    ).astype(jnp.bfloat16)
    up_grad = (inner_grad * activated).astype(jnp.bfloat16)
    gate_wgrad = jnp.einsum("tc,tf->cf", hidden_two, gate_grad, preferred_element_type=jnp.float32)
    up_wgrad = jnp.einsum("tc,tf->cf", hidden_two, up_grad, preferred_element_type=jnp.float32)
    hidden_two_part = jnp.einsum(
        "tf,cf->tc", gate_grad, gate_back, preferred_element_type=jnp.float32
    ) + jnp.einsum("tf,cf->tc", up_grad, up_back, preferred_element_type=jnp.float32)
    hidden_two_grad = lax.psum(hidden_two_part.astype(jnp.bfloat16), "tp").astype(jnp.float32)
    ffn_gain_grad = jnp.sum(hidden_two_grad * normed_two, axis=0)
    middle_grad = grad_out.astype(jnp.float32) + norm_back(
        hidden_two_grad, normed_two, factor_two, gain_ffn_back.astype(jnp.float32)
    )
    branch_low = middle_grad.astype(jnp.bfloat16)
    out_wgrad = jnp.einsum("ta,td->ad", mixed_low, branch_low, preferred_element_type=jnp.float32)
    mixed_grad = jnp.einsum(
        "td,ad->ta", branch_low, out_back, preferred_element_type=jnp.float32
    ).astype(jnp.bfloat16)
    attended_grad = to_heads(mixed_grad, sequences, key_heads, group_size)
    delta = jnp.sum(attended_grad.astype(jnp.float32) * attended, axis=-1)

    def cycle_turn(turn, cycle_state):
        query_grad, key_now, value_now, key_grad, value_grad = cycle_state
        source = (own_index - turn) % ctx_count
        place_now = lax.dynamic_index_in_dim(every_place, source, 0, keepdims=False)
        scores = scores_for(key_now, place_now)
        weights = jnp.exp(scores - log_total[..., None])
        value_grad = value_grad + jnp.einsum(
            "shrk,shrd->shkd",
            weights.astype(jnp.bfloat16),
            attended_grad,
            preferred_element_type=jnp.float32,
        )
        weight_grad = jnp.einsum(
            "shrd,shkd->shrk", attended_grad, value_now, preferred_element_type=jnp.float32
        )
        score_grad = (weights * (weight_grad - delta[..., None])).astype(jnp.bfloat16)
        query_grad = (
            query_grad
            + jnp.einsum("shrk,shkd->shrd", score_grad, key_now, preferred_element_type=jnp.float32)
            * SCALE
        )
        key_grad = (
            key_grad
            + jnp.einsum("shrk,shrd->shkd", score_grad, queries, preferred_element_type=jnp.float32)
            * SCALE
        )
        key_now, value_now = passed_along((key_now, value_now), "ctx", 1)
        key_grad, value_grad = (
            passed_along(key_grad.astype(jnp.bfloat16), "ctx", 1).astype(key_grad.dtype),
            passed_along(value_grad.astype(jnp.bfloat16), "ctx", 1).astype(value_grad.dtype),
        )
        return (query_grad, key_now, value_now, key_grad, value_grad)

    cycle_start = (
        jnp.zeros(attended.shape, jnp.float32),
        keys,
        values,
        jnp.zeros(keys.shape, jnp.float32),
        jnp.zeros(keys.shape, jnp.float32),
    )
    query_grad, key_home, value_home, key_grad, value_grad = lax.fori_loop(
        0, ctx_count, cycle_turn, cycle_start
    )
    query_rot_grad = from_heads(query_grad, group_size).reshape(token_rows, query_heads, DH)
    key_rot_grad = from_heads(key_grad, 1).reshape(token_rows, key_heads, DH)
    value_grad_low = from_heads(value_grad, 1).astype(jnp.bfloat16)
    query_out_grad = rotate(query_rot_grad, cosine, -sine_part)
    key_out_grad = rotate(key_rot_grad, cosine, -sine_part)
    query_gain_grad = jnp.sum(query_out_grad * query_normed, axis=(0, 1))
    key_gain_grad = jnp.sum(key_out_grad * key_normed, axis=(0, 1))
    query_pre_grad = (
        norm_back(query_out_grad, query_normed, query_factor, gain_query_back.astype(jnp.float32))
        .reshape(token_rows, query_heads * DH)
        .astype(jnp.bfloat16)
    )
    key_pre_grad = (
        norm_back(key_out_grad, key_normed, key_factor, gain_key_back.astype(jnp.float32))
        .reshape(token_rows, key_heads * DH)
        .astype(jnp.bfloat16)
    )
    query_wgrad = jnp.einsum(
        "tc,ta->ca", hidden_one, query_pre_grad, preferred_element_type=jnp.float32
    )
    key_wgrad = jnp.einsum(
        "tc,ta->ca", hidden_one, key_pre_grad, preferred_element_type=jnp.float32
    )
    value_wgrad = jnp.einsum(
        "tc,ta->ca", hidden_one, value_grad_low, preferred_element_type=jnp.float32
    )
    hidden_one_part = (
        jnp.einsum("ta,ca->tc", query_pre_grad, query_back, preferred_element_type=jnp.float32)
        + jnp.einsum("ta,ca->tc", key_pre_grad, key_back, preferred_element_type=jnp.float32)
        + jnp.einsum("ta,ca->tc", value_grad_low, value_back, preferred_element_type=jnp.float32)
    )
    hidden_one_grad, query_gain_sum, key_gain_sum = (
        lax.psum(hidden_one_part.astype(jnp.bfloat16), "tp").astype(jnp.float32),
        lax.psum(query_gain_grad.astype(jnp.bfloat16), "tp").astype(jnp.float32),
        lax.psum(key_gain_grad.astype(jnp.bfloat16), "tp").astype(jnp.float32),
    )
    attn_gain_grad = jnp.sum(hidden_one_grad * normed_one, axis=0)
    states_grad = middle_grad + norm_back(
        hidden_one_grad, normed_one, factor_one, gain_attn_back.astype(jnp.float32)
    )
    shares = (
        lax.psum_scatter(
            attn_gain_grad.astype(jnp.bfloat16), "ctx", scatter_dimension=0, tiled=True
        ).astype(jnp.float32),
        lax.psum_scatter(
            query_wgrad.astype(jnp.bfloat16), "ctx", scatter_dimension=0, tiled=True
        ).astype(jnp.float32),
        lax.psum_scatter(
            key_wgrad.astype(jnp.bfloat16), "ctx", scatter_dimension=0, tiled=True
        ).astype(jnp.float32),
        lax.psum_scatter(
            value_wgrad.astype(jnp.bfloat16), "ctx", scatter_dimension=0, tiled=True
        ).astype(jnp.float32),
        lax.psum_scatter(
            query_gain_sum.astype(jnp.bfloat16), "ctx", scatter_dimension=0, tiled=True
        ).astype(jnp.float32),
        lax.psum_scatter(
            key_gain_sum.astype(jnp.bfloat16), "ctx", scatter_dimension=0, tiled=True
        ).astype(jnp.float32),
        lax.psum_scatter(
            out_wgrad.astype(jnp.bfloat16), "ctx", scatter_dimension=1, tiled=True
        ).astype(jnp.float32),
        lax.psum_scatter(
            ffn_gain_grad.astype(jnp.bfloat16), "ctx", scatter_dimension=0, tiled=True
        ).astype(jnp.float32),
        lax.psum_scatter(
            gate_wgrad.astype(jnp.bfloat16), "ctx", scatter_dimension=0, tiled=True
        ).astype(jnp.float32),
        lax.psum_scatter(
            up_wgrad.astype(jnp.bfloat16), "ctx", scatter_dimension=0, tiled=True
        ).astype(jnp.float32),
        lax.psum_scatter(
            down_grad.astype(jnp.bfloat16), "ctx", scatter_dimension=1, tiled=True
        ).astype(jnp.float32),
    )
    return (
        output_low,
        states_grad,
        shares[0],
        shares[1],
        shares[2],
        shares[3],
        shares[4],
        shares[5],
        shares[6],
        shares[7],
        shares[8],
        shares[9],
        shares[10],
    )


def solution(mesh):
    in_specs = (
        P("ctx", None),
        P("ctx", None),
        P("ctx"),
        P("ctx", "tp"),
        P("ctx", "tp"),
        P("ctx", "tp"),
        P("ctx"),
        P("ctx"),
        P("tp", "ctx"),
        P("ctx"),
        P("ctx", "tp"),
        P("ctx", "tp"),
        P("tp", "ctx"),
        P("ctx", None),
    )
    out_specs = (
        P("ctx", None),
        P("ctx", None),
        P("ctx"),
        P("ctx", "tp"),
        P("ctx", "tp"),
        P("ctx", "tp"),
        P("ctx"),
        P("ctx"),
        P("tp", "ctx"),
        P("ctx"),
        P("ctx", "tp"),
        P("ctx", "tp"),
        P("tp", "ctx"),
    )
    return jax.shard_map(shards, mesh=mesh, in_specs=in_specs, out_specs=out_specs, check_vma=False)
```

profile of v0, /device:TPU:0, one launch (start us, length us, event | category | flops | bytes accessed | tf_op | source)
XLA Modules:
  0.0 1258.7 jit_solution(4828087074399001518)
XLA Ops:
  8.0 23.1 %all-gather.2 = s32[16,1,4]{2,1,0:T(1,128)S(1)} all-gather(s32[1,1,4]{2,1,0:T(1,128)} %bitcast.246), channel_id=1, replica_groups=mesh['ctx'=16,'tp'=2] {'ctx'}, dimensions={0}, use_global_device_ids=true | all-gather | bytes 272 | tf_op jit(solution)/shard_map/all_gather | solution.py:88
  37.6 30.3 %all-reduce.9 = (bf16[1024]{0:T(1024)(128)(2,1)S(1)}, bf16[64]{0:T(256)(128)(2,1)S(1)}, bf16[64]{0:T(256)(128)(2,1)S(1)}, bf16[1024]{0:T(1024)(128)(2,1)S(1)}) all-reduce(bf16[1024]{0:T(1024)(128)(2,1)S(1)} %dynamic-update-slice, bf16[64]{0:T(256)(128)(2,1)S(1)} %dynamic-update-slice.1, ...), channel_id=1, replica_groups=mesh['ctx'=16,'tp'=2] {'ctx'}, use_global_device_ids=true, to_apply=%add | all-reduce | flops 2176 | bytes 8704
  71.0 19.0 %all_gather.55 = bf16[1024,256]{1,0:T(8,128)(2,1)S(1)} all-gather(bf16[64,256]{1,0:T(8,128)(2,1)} %param.22), channel_id=1, replica_groups=mesh['ctx'=16,'tp'=2] {'ctx'}, dimensions={0}, use_global_device_ids=true | all-gather | bytes 557056 | tf_op jit(solution)/shard_map/all_gather | solution.py:98
  93.6 20.5 %all_gather.60 = bf16[1024,256]{1,0:T(8,128)(2,1)S(1)} all-gather(bf16[64,256]{1,0:T(8,128)(2,1)S(1)} %copy-done.42), channel_id=1, replica_groups=mesh['ctx'=16,'tp'=2] {'ctx'}, dimensions={0}, use_global_device_ids=true | all-gather | bytes 557056 | tf_op jit(solution)/shard_map/all_gather | solution.py:99
  120.0 21.2 %all-gather.21.cloned.1.call-done = bf16[2,4,1,2048,64]{3,0,4,1,2:T(2,128)(2,1)} async-done(((bf16[2,4,1,128,64]{3,0,4,1,2:T(2,128)(2,1)}), bf16[2,4,1,2048,64]{3,0,4,1,2:T(2,128)(2,1)}) %all-gather.21.cloned.1.call-update) | async-done | bytes 2097168 | tf_op jit(solution)/shard_map/all_gather | solution.py:163
  141.2 4.4 reshape.313
  145.6 3.7 copy.173
  149.3 42.1 %all-gather.23.cloned.1.call-done = bf16[2,4,1,2048,64]{3,0,4,1,2:T(2,128)(2,1)} async-done(((bf16[2,4,1,128,64]{3,0,4,1,2:T(2,128)(2,1)}), bf16[2,4,1,2048,64]{3,0,4,1,2:T(2,128)(2,1)}) %all-gather.23.cloned.1.call-update) | async-done | bytes 2097168 | tf_op jit(solution)/shard_map/all_gather | solution.py:164
  191.4 4.4 reshape.318
  199.5 66.6 %while.39 = (s32[]{:T(128)}, f32[2,4,256]{2,1,0:T(4,128)S(1)}, f32[2,4,256]{2,1,0:T(4,128)S(1)}, f32[2,4,256,64]{2,3,1,0:T(8,128)S(1)}, s32[16,2,128]{2,1,0:T(2,...) while((s32[]{:T(128)}, f32[2,4,256]{2,1,0:T(4,128)S(1)}, ...), condition=%wide.region_6.7_spmd.clone, body=%wide.region_3.6_spmd.clone.sunk | while | flops 69412864 | bytes 4993165 | solution.py:192
  274.5 23.3 %all-reduce.16.cloned.1.call-done = bf16[256,1024]{1,0:T(8,128)(2,1)} async-done(((bf16[256,1024]{1,0:T(8,128)(2,1)}), bf16[256,1024]{1,0:T(8,128)(2,1)}) %all-reduce.16.cloned.1.call-update) | async-done | bytes 524304 | tf_op jit(solution)/shard_map/psum | solution.py:198
  300.4 53.1 %all-gather.15.cloned.1.call-done = bf16[1024,2304]{1,0:T(8,128)(2,1)} async-done(((bf16[64,2304]{1,0:T(8,128)(2,1)}), bf16[1024,2304]{1,0:T(8,128)(2,1)}) %all-gather.15.cloned.1.call-update) | async-done | bytes 4718608 | tf_op jit(solution)/shard_map/all_gather | solution.py:104
  353.5 5.1 fusion.75
  358.6 49.3 %all-gather.17.cloned.1.call-done = bf16[1024,2304]{1,0:T(8,128)(2,1)} async-done(((bf16[64,2304]{1,0:T(8,128)(2,1)}), bf16[1024,2304]{1,0:T(8,128)(2,1)}) %all-gather.17.cloned.1.call-update) | async-done | bytes 4718608 | tf_op jit(solution)/shard_map/all_gather | solution.py:105
  407.9 5.1 fusion.76
  413.0 49.2 %all-gather.19.cloned.1.call-done = bf16[2304,1024]{0,1:T(8,128)(2,1)} async-done(((bf16[2304,64]{0,1:T(8,128)(2,1)}), bf16[2304,1024]{0,1:T(8,128)(2,1)}) %all-gather.19.cloned.1.call-update) | async-done | bytes 4718608 | tf_op jit(solution)/shard_map/all_gather | solution.py:106
  462.2 6.6 multiply_convert_fusion
  468.8 4.6 fusion.77
  476.7 5.0 convolution_convert_fusion.7
  481.6 21.5 %all-reduce.18.cloned.1.call-done = bf16[256,1024]{1,0:T(8,128)(2,1)} async-done(((bf16[256,1024]{1,0:T(8,128)(2,1)}), bf16[256,1024]{1,0:T(8,128)(2,1)}) %all-reduce.18.cloned.1.call-update) | async-done | bytes 524304 | tf_op jit(solution)/shard_map/psum | solution.py:247
  513.7 215.4 %while.40 = (s32[]{:T(128)}, f32[2,4,256,64]{2,3,1,0:T(8,128)S(1)}, bf16[2,4,128,64]{2,3,1,0:T(8,128)(2,1)S(1)}, bf16[2,4,128,64]{2,3,1,0:T(8,128)(2,1)S(1)}, f3...) while((s32[]{:T(128)}, f32[2,4,256,64]{2,3,1,0:T(8,128)S(1)}, ...), condition=%wide.region_14.15_spmd.clone, body=%wide.region_13.14_spmd.clone.sunk | while | flops 170655760 | bytes 11563496 | solution.py:300
  521.2 4.8 collective-permute-done.2
  534.3 5.2 collective-permute-done.2
  546.5 6.3 collective-permute-done.2
  559.8 6.5 collective-permute-done.2
  573.2 6.5 collective-permute-done.2
  586.5 6.5 collective-permute-done.2
  599.9 6.5 collective-permute-done.2
  613.3 6.5 collective-permute-done.2
  626.6 6.5 collective-permute-done.2
  640.0 6.5 collective-permute-done.2
  653.4 6.5 collective-permute-done.2
  666.8 6.5 collective-permute-done.2
  680.1 6.5 collective-permute-done.2
  693.5 6.5 collective-permute-done.2
  706.8 6.5 collective-permute-done.2
  720.2 6.5 collective-permute-done.2
  747.9 4.9 convolution_convert_fusion.2
  764.3 26.9 %reduce-scatter.10.cloned.1.call-done = bf16[64,256]{1,0:T(8,128)(2,1)} async-done(((bf16[1024,256]{1,0:T(8,128)(2,1)}), bf16[64,256]{1,0:T(8,128)(2,1)}) %reduce-scatter.10.cloned.1.call-update) | async-done | bytes 32784 | tf_op jit(solution)/shard_map/reduce_scatter | solution.py:350
  792.6 41.5 %all-reduce.20.cloned.1.call-done = (bf16[256,1024]{1,0:T(8,128)(2,1)}, bf16[256,1024]{1,0:T(8,128)(2,1)}) async-done(((bf16[256,1024]{1,0:T(8,128)(2,1)}, bf16[256,1024]{1,0:T(8,128)(2,1)}), (bf16[256,1024]{1,0:T(8,128)(2,1)}, bf16[256,1024]{1,0:T(8,128)(2,1)})) %all-reduce.20.cloned.1.call-update) | async-done | bytes 1048592 | tf_op jit(solution)/shard_map/psum | solution.py:208
  835.6 33.7 %all-reduce.8 = (bf16[1024]{0:T(1024)(128)(2,1)S(1)}, bf16[64]{0:T(256)(128)(2,1)S(1)}, bf16[64]{0:T(256)(128)(2,1)S(1)}, bf16[1024]{0:T(1024)(128)(2,1)S(1)}) all-reduce(bf16[1024]{0:T(1024)(128)(2,1)S(1)} %get-tuple-element.524, bf16[64]{0:T(256)(128)(2,1)S(1)} %reduce_sum.152, ...), channel_id=4, replica_groups=mesh['ctx'=16,'tp'=2] {'ctx'}, use_global_device_ids=true, to_apply=%region_20.21.clone | all-reduce | flops 2176 | bytes 8704
  869.4 24.4 %reduce-scatter.12.cloned.1.call-done = bf16[64,256]{1,0:T(8,128)(2,1)} async-done(((bf16[1024,256]{1,0:T(8,128)(2,1)}), bf16[64,256]{1,0:T(8,128)(2,1)}) %reduce-scatter.12.cloned.1.call-update) | async-done | bytes 32784 | tf_op jit(solution)/shard_map/reduce_scatter | solution.py:353
  895.2 4.9 all-reduce.10
  904.9 49.5 %reduce-scatter.8.cloned.1.call-done = bf16[64,512]{1,0:T(8,128)(2,1)} async-done(((bf16[1024,512]{1,0:T(8,128)(2,1)}), bf16[64,512]{1,0:T(8,128)(2,1)}) %reduce-scatter.8.cloned.1.call-update) | async-done | bytes 65552 | tf_op jit(solution)/shard_map/reduce_scatter | solution.py:347
  955.9 58.5 %reduce-scatter.14.cloned.1.call-done = bf16[512,64]{0,1:T(8,128)(2,1)} async-done(((bf16[512,1024]{0,1:T(8,128)(2,1)}), bf16[512,64]{0,1:T(8,128)(2,1)}) %reduce-scatter.14.cloned.1.call-update) | async-done | bytes 65552 | tf_op jit(solution)/shard_map/reduce_scatter | solution.py:362
  1015.8 77.3 %reduce-scatter.16.cloned.1.call-done = bf16[64,2304]{1,0:T(8,128)(2,1)} async-done(((bf16[1024,2304]{1,0:T(8,128)(2,1)}), bf16[64,2304]{1,0:T(8,128)(2,1)}) %reduce-scatter.16.cloned.1.call-update) | async-done | bytes 294928 | tf_op jit(solution)/shard_map/reduce_scatter | solution.py:368
  1094.9 76.6 %reduce-scatter.18.cloned.1.call-done = bf16[64,2304]{1,0:T(8,128)(2,1)} async-done(((bf16[1024,2304]{1,0:T(8,128)(2,1)}), bf16[64,2304]{1,0:T(8,128)(2,1)}) %reduce-scatter.18.cloned.1.call-update) | async-done | bytes 294928 | tf_op jit(solution)/shard_map/reduce_scatter | solution.py:371
  1173.3 77.0 %reduce-scatter.20.cloned.1.call-done = bf16[2304,64]{0,1:T(8,128)(2,1)} async-done(((bf16[2304,1024]{0,1:T(8,128)(2,1)}), bf16[2304,64]{0,1:T(8,128)(2,1)}) %reduce-scatter.20.cloned.1.call-update) | async-done | bytes 294928 | tf_op jit(solution)/shard_map/reduce_scatter | solution.py:374
  (764 shorter events, 270.5 us)
Async XLA Ops:
  7.2 109.6 %all-gather.11.cloned.1.call-start = ((), (), s32[]{:S(2)}) async-start(), calls=%async_computation.7 | async-start | bytes 1114112 | tf_op jit(solution)/shard_map/all_gather | solution.py:97
  7.9 133.3 %all-gather.21.cloned.1.call-start = ((), (), s32[]{:S(2)}) async-start(), calls=%async_computation.21 | async-start | bytes 2228224 | tf_op jit(solution)/shard_map/all_gather | solution.py:163
  93.5 97.9 %all-gather.23.cloned.1.call-start = ((), (), s32[]{:S(2)}) async-start(), calls=%async_computation.22 | async-start | bytes 2228224 | tf_op jit(solution)/shard_map/all_gather | solution.py:164
  116.1 150.4 %all-gather.13.cloned.1.call-start = ((), (), s32[]{:S(2)}) async-start(), calls=%async_computation.8 | async-start | bytes 1114112 | tf_op jit(solution)/shard_map/all_gather | solution.py:102
  116.7 181.2 %all-reduce.16.cloned.1.call-start = ((), (), s32[]{:S(2)}) async-start(), calls=%async_computation.9 | async-start | bytes 1048576 | tf_op jit(solution)/shard_map/psum | solution.py:198
  269.2 84.3 %all-gather.15.cloned.1.call-start = ((), (), s32[]{:S(2)}) async-start(), calls=%async_computation.10 | async-start | bytes 5013504 | tf_op jit(solution)/shard_map/all_gather | solution.py:104
  269.7 138.1 %all-gather.17.cloned.1.call-start = ((), (), s32[]{:S(2)}) async-start(), calls=%async_computation.11 | async-start | bytes 5013504 | tf_op jit(solution)/shard_map/all_gather | solution.py:105
  270.5 191.7 %all-gather.19.cloned.1.call-start = ((), (), s32[]{:S(2)}) async-start(), calls=%async_computation.12 | async-start | bytes 5013504 | tf_op jit(solution)/shard_map/all_gather | solution.py:106
  271.2 231.8 %all-reduce.18.cloned.1.call-start = ((), (), s32[]{:S(2)}) async-start(), calls=%async_computation.13 | async-start | bytes 1048576 | tf_op jit(solution)/shard_map/psum | solution.py:247
  475.8 315.4 %reduce-scatter.10.cloned.1.call-start = ((), (), s32[]{:S(2)}) async-start(), calls=%async_computation.15 | async-start | bytes 557056 | tf_op jit(solution)/shard_map/reduce_scatter | solution.py:350
  513.7 14.8 %collective-permute-start = (bf16[2,4,128,64]{2,3,1,0:T(8,128)(2,1)S(1)}, bf16[2,4,128,64]{2,3,1,0:T(8,128)(2,1)S(1)}, u32[]{:S(2)}, u32[]{:S(2)}) collective-permute-start(bf16[2,4,128,64]{2,3,1,0:T(8,128)(2,1)S(1)} %copy.206), channel_id=1, source_target_pairs={{0,2},{2,4},{4,6},{6,8},{8,10},{10,12},{12,14},{14,16},{16,18},{18... | collective-permute-start | bytes 393224 | tf_op jit(solution)/shard_map/while/body/eval_jaxpr/ppermute | solution.py:18
  513.8 14.7 %collective-permute-start.1 = (bf16[2,4,128,64]{2,3,1,0:T(8,128)(2,1)S(1)}, bf16[2,4,128,64]{2,3,1,0:T(8,128)(2,1)S(1)}, u32[]{:S(2)}, u32[]{:S(2)}) collective-permute-start(bf16[2,4,128,64]{2,3,1,0:T(8,128)(2,1)S(1)} %copy.207), channel_id=1, source_target_pairs={{0,2},{2,4},{4,6},{6,8},{8,10},{10,12},{12,14},{14,16},{16,18},{18... | collective-permute-start | bytes 393224 | tf_op jit(solution)/shard_map/while/body/eval_jaxpr/ppermute | solution.py:18
  528.6 13.3 %collective-permute-start = (bf16[2,4,128,64]{2,3,1,0:T(8,128)(2,1)S(1)}, bf16[2,4,128,64]{2,3,1,0:T(8,128)(2,1)S(1)}, u32[]{:S(2)}, u32[]{:S(2)}) collective-permute-start(bf16[2,4,128,64]{2,3,1,0:T(8,128)(2,1)S(1)} %copy.206), channel_id=1, source_target_pairs={{0,2},{2,4},{4,6},{6,8},{8,10},{10,12},{12,14},{14,16},{16,18},{18... | collective-permute-start | bytes 393224 | tf_op jit(solution)/shard_map/while/body/eval_jaxpr/ppermute | solution.py:18
  528.7 13.3 %collective-permute-start.1 = (bf16[2,4,128,64]{2,3,1,0:T(8,128)(2,1)S(1)}, bf16[2,4,128,64]{2,3,1,0:T(8,128)(2,1)S(1)}, u32[]{:S(2)}, u32[]{:S(2)}) collective-permute-start(bf16[2,4,128,64]{2,3,1,0:T(8,128)(2,1)S(1)} %copy.207), channel_id=1, source_target_pairs={{0,2},{2,4},{4,6},{6,8},{8,10},{10,12},{12,14},{14,16},{16,18},{18... | collective-permute-start | bytes 393224 | tf_op jit(solution)/shard_map/while/body/eval_jaxpr/ppermute | solution.py:18
  542.0 13.3 %collective-permute-start = (bf16[2,4,128,64]{2,3,1,0:T(8,128)(2,1)S(1)}, bf16[2,4,128,64]{2,3,1,0:T(8,128)(2,1)S(1)}, u32[]{:S(2)}, u32[]{:S(2)}) collective-permute-start(bf16[2,4,128,64]{2,3,1,0:T(8,128)(2,1)S(1)} %copy.206), channel_id=1, source_target_pairs={{0,2},{2,4},{4,6},{6,8},{8,10},{10,12},{12,14},{14,16},{16,18},{18... | collective-permute-start | bytes 393224 | tf_op jit(solution)/shard_map/while/body/eval_jaxpr/ppermute | solution.py:18
  542.0 13.2 %collective-permute-start.1 = (bf16[2,4,128,64]{2,3,1,0:T(8,128)(2,1)S(1)}, bf16[2,4,128,64]{2,3,1,0:T(8,128)(2,1)S(1)}, u32[]{:S(2)}, u32[]{:S(2)}) collective-permute-start(bf16[2,4,128,64]{2,3,1,0:T(8,128)(2,1)S(1)} %copy.207), channel_id=1, source_target_pairs={{0,2},{2,4},{4,6},{6,8},{8,10},{10,12},{12,14},{14,16},{16,18},{18... | collective-permute-start | bytes 393224 | tf_op jit(solution)/shard_map/while/body/eval_jaxpr/ppermute | solution.py:18
  555.3 13.3 %collective-permute-start = (bf16[2,4,128,64]{2,3,1,0:T(8,128)(2,1)S(1)}, bf16[2,4,128,64]{2,3,1,0:T(8,128)(2,1)S(1)}, u32[]{:S(2)}, u32[]{:S(2)}) collective-permute-start(bf16[2,4,128,64]{2,3,1,0:T(8,128)(2,1)S(1)} %copy.206), channel_id=1, source_target_pairs={{0,2},{2,4},{4,6},{6,8},{8,10},{10,12},{12,14},{14,16},{16,18},{18... | collective-permute-start | bytes 393224 | tf_op jit(solution)/shard_map/while/body/eval_jaxpr/ppermute | solution.py:18
  555.4 13.3 %collective-permute-start.1 = (bf16[2,4,128,64]{2,3,1,0:T(8,128)(2,1)S(1)}, bf16[2,4,128,64]{2,3,1,0:T(8,128)(2,1)S(1)}, u32[]{:S(2)}, u32[]{:S(2)}) collective-permute-start(bf16[2,4,128,64]{2,3,1,0:T(8,128)(2,1)S(1)} %copy.207), channel_id=1, source_target_pairs={{0,2},{2,4},{4,6},{6,8},{8,10},{10,12},{12,14},{14,16},{16,18},{18... | collective-permute-start | bytes 393224 | tf_op jit(solution)/shard_map/while/body/eval_jaxpr/ppermute | solution.py:18
  568.7 13.3 %collective-permute-start = (bf16[2,4,128,64]{2,3,1,0:T(8,128)(2,1)S(1)}, bf16[2,4,128,64]{2,3,1,0:T(8,128)(2,1)S(1)}, u32[]{:S(2)}, u32[]{:S(2)}) collective-permute-start(bf16[2,4,128,64]{2,3,1,0:T(8,128)(2,1)S(1)} %copy.206), channel_id=1, source_target_pairs={{0,2},{2,4},{4,6},{6,8},{8,10},{10,12},{12,14},{14,16},{16,18},{18... | collective-permute-start | bytes 393224 | tf_op jit(solution)/shard_map/while/body/eval_jaxpr/ppermute | solution.py:18
  568.8 13.3 %collective-permute-start.1 = (bf16[2,4,128,64]{2,3,1,0:T(8,128)(2,1)S(1)}, bf16[2,4,128,64]{2,3,1,0:T(8,128)(2,1)S(1)}, u32[]{:S(2)}, u32[]{:S(2)}) collective-permute-start(bf16[2,4,128,64]{2,3,1,0:T(8,128)(2,1)S(1)} %copy.207), channel_id=1, source_target_pairs={{0,2},{2,4},{4,6},{6,8},{8,10},{10,12},{12,14},{14,16},{16,18},{18... | collective-permute-start | bytes 393224 | tf_op jit(solution)/shard_map/while/body/eval_jaxpr/ppermute | solution.py:18
  582.1 13.3 %collective-permute-start = (bf16[2,4,128,64]{2,3,1,0:T(8,128)(2,1)S(1)}, bf16[2,4,128,64]{2,3,1,0:T(8,128)(2,1)S(1)}, u32[]{:S(2)}, u32[]{:S(2)}) collective-permute-start(bf16[2,4,128,64]{2,3,1,0:T(8,128)(2,1)S(1)} %copy.206), channel_id=1, source_target_pairs={{0,2},{2,4},{4,6},{6,8},{8,10},{10,12},{12,14},{14,16},{16,18},{18... | collective-permute-start | bytes 393224 | tf_op jit(solution)/shard_map/while/body/eval_jaxpr/ppermute | solution.py:18
  582.2 13.2 %collective-permute-start.1 = (bf16[2,4,128,64]{2,3,1,0:T(8,128)(2,1)S(1)}, bf16[2,4,128,64]{2,3,1,0:T(8,128)(2,1)S(1)}, u32[]{:S(2)}, u32[]{:S(2)}) collective-permute-start(bf16[2,4,128,64]{2,3,1,0:T(8,128)(2,1)S(1)} %copy.207), channel_id=1, source_target_pairs={{0,2},{2,4},{4,6},{6,8},{8,10},{10,12},{12,14},{14,16},{16,18},{18... | collective-permute-start | bytes 393224 | tf_op jit(solution)/shard_map/while/body/eval_jaxpr/ppermute | solution.py:18
  595.5 13.3 %collective-permute-start = (bf16[2,4,128,64]{2,3,1,0:T(8,128)(2,1)S(1)}, bf16[2,4,128,64]{2,3,1,0:T(8,128)(2,1)S(1)}, u32[]{:S(2)}, u32[]{:S(2)}) collective-permute-start(bf16[2,4,128,64]{2,3,1,0:T(8,128)(2,1)S(1)} %copy.206), channel_id=1, source_target_pairs={{0,2},{2,4},{4,6},{6,8},{8,10},{10,12},{12,14},{14,16},{16,18},{18... | collective-permute-start | bytes 393224 | tf_op jit(solution)/shard_map/while/body/eval_jaxpr/ppermute | solution.py:18
  595.5 13.2 %collective-permute-start.1 = (bf16[2,4,128,64]{2,3,1,0:T(8,128)(2,1)S(1)}, bf16[2,4,128,64]{2,3,1,0:T(8,128)(2,1)S(1)}, u32[]{:S(2)}, u32[]{:S(2)}) collective-permute-start(bf16[2,4,128,64]{2,3,1,0:T(8,128)(2,1)S(1)} %copy.207), channel_id=1, source_target_pairs={{0,2},{2,4},{4,6},{6,8},{8,10},{10,12},{12,14},{14,16},{16,18},{18... | collective-permute-start | bytes 393224 | tf_op jit(solution)/shard_map/while/body/eval_jaxpr/ppermute | solution.py:18
  608.8 13.3 %collective-permute-start = (bf16[2,4,128,64]{2,3,1,0:T(8,128)(2,1)S(1)}, bf16[2,4,128,64]{2,3,1,0:T(8,128)(2,1)S(1)}, u32[]{:S(2)}, u32[]{:S(2)}) collective-permute-start(bf16[2,4,128,64]{2,3,1,0:T(8,128)(2,1)S(1)} %copy.206), channel_id=1, source_target_pairs={{0,2},{2,4},{4,6},{6,8},{8,10},{10,12},{12,14},{14,16},{16,18},{18... | collective-permute-start | bytes 393224 | tf_op jit(solution)/shard_map/while/body/eval_jaxpr/ppermute | solution.py:18
  608.9 13.3 %collective-permute-start.1 = (bf16[2,4,128,64]{2,3,1,0:T(8,128)(2,1)S(1)}, bf16[2,4,128,64]{2,3,1,0:T(8,128)(2,1)S(1)}, u32[]{:S(2)}, u32[]{:S(2)}) collective-permute-start(bf16[2,4,128,64]{2,3,1,0:T(8,128)(2,1)S(1)} %copy.207), channel_id=1, source_target_pairs={{0,2},{2,4},{4,6},{6,8},{8,10},{10,12},{12,14},{14,16},{16,18},{18... | collective-permute-start | bytes 393224 | tf_op jit(solution)/shard_map/while/body/eval_jaxpr/ppermute | solution.py:18
  622.2 13.3 %collective-permute-start = (bf16[2,4,128,64]{2,3,1,0:T(8,128)(2,1)S(1)}, bf16[2,4,128,64]{2,3,1,0:T(8,128)(2,1)S(1)}, u32[]{:S(2)}, u32[]{:S(2)}) collective-permute-start(bf16[2,4,128,64]{2,3,1,0:T(8,128)(2,1)S(1)} %copy.206), channel_id=1, source_target_pairs={{0,2},{2,4},{4,6},{6,8},{8,10},{10,12},{12,14},{14,16},{16,18},{18... | collective-permute-start | bytes 393224 | tf_op jit(solution)/shard_map/while/body/eval_jaxpr/ppermute | solution.py:18
  622.3 13.2 %collective-permute-start.1 = (bf16[2,4,128,64]{2,3,1,0:T(8,128)(2,1)S(1)}, bf16[2,4,128,64]{2,3,1,0:T(8,128)(2,1)S(1)}, u32[]{:S(2)}, u32[]{:S(2)}) collective-permute-start(bf16[2,4,128,64]{2,3,1,0:T(8,128)(2,1)S(1)} %copy.207), channel_id=1, source_target_pairs={{0,2},{2,4},{4,6},{6,8},{8,10},{10,12},{12,14},{14,16},{16,18},{18... | collective-permute-start | bytes 393224 | tf_op jit(solution)/shard_map/while/body/eval_jaxpr/ppermute | solution.py:18
  635.6 13.3 %collective-permute-start = (bf16[2,4,128,64]{2,3,1,0:T(8,128)(2,1)S(1)}, bf16[2,4,128,64]{2,3,1,0:T(8,128)(2,1)S(1)}, u32[]{:S(2)}, u32[]{:S(2)}) collective-permute-start(bf16[2,4,128,64]{2,3,1,0:T(8,128)(2,1)S(1)} %copy.206), channel_id=1, source_target_pairs={{0,2},{2,4},{4,6},{6,8},{8,10},{10,12},{12,14},{14,16},{16,18},{18... | collective-permute-start | bytes 393224 | tf_op jit(solution)/shard_map/while/body/eval_jaxpr/ppermute | solution.py:18
  635.7 13.3 %collective-permute-start.1 = (bf16[2,4,128,64]{2,3,1,0:T(8,128)(2,1)S(1)}, bf16[2,4,128,64]{2,3,1,0:T(8,128)(2,1)S(1)}, u32[]{:S(2)}, u32[]{:S(2)}) collective-permute-start(bf16[2,4,128,64]{2,3,1,0:T(8,128)(2,1)S(1)} %copy.207), channel_id=1, source_target_pairs={{0,2},{2,4},{4,6},{6,8},{8,10},{10,12},{12,14},{14,16},{16,18},{18... | collective-permute-start | bytes 393224 | tf_op jit(solution)/shard_map/while/body/eval_jaxpr/ppermute | solution.py:18
  649.0 13.3 %collective-permute-start = (bf16[2,4,128,64]{2,3,1,0:T(8,128)(2,1)S(1)}, bf16[2,4,128,64]{2,3,1,0:T(8,128)(2,1)S(1)}, u32[]{:S(2)}, u32[]{:S(2)}) collective-permute-start(bf16[2,4,128,64]{2,3,1,0:T(8,128)(2,1)S(1)} %copy.206), channel_id=1, source_target_pairs={{0,2},{2,4},{4,6},{6,8},{8,10},{10,12},{12,14},{14,16},{16,18},{18... | collective-permute-start | bytes 393224 | tf_op jit(solution)/shard_map/while/body/eval_jaxpr/ppermute | solution.py:18
  649.0 13.3 %collective-permute-start.1 = (bf16[2,4,128,64]{2,3,1,0:T(8,128)(2,1)S(1)}, bf16[2,4,128,64]{2,3,1,0:T(8,128)(2,1)S(1)}, u32[]{:S(2)}, u32[]{:S(2)}) collective-permute-start(bf16[2,4,128,64]{2,3,1,0:T(8,128)(2,1)S(1)} %copy.207), channel_id=1, source_target_pairs={{0,2},{2,4},{4,6},{6,8},{8,10},{10,12},{12,14},{14,16},{16,18},{18... | collective-permute-start | bytes 393224 | tf_op jit(solution)/shard_map/while/body/eval_jaxpr/ppermute | solution.py:18
  662.3 13.3 %collective-permute-start = (bf16[2,4,128,64]{2,3,1,0:T(8,128)(2,1)S(1)}, bf16[2,4,128,64]{2,3,1,0:T(8,128)(2,1)S(1)}, u32[]{:S(2)}, u32[]{:S(2)}) collective-permute-start(bf16[2,4,128,64]{2,3,1,0:T(8,128)(2,1)S(1)} %copy.206), channel_id=1, source_target_pairs={{0,2},{2,4},{4,6},{6,8},{8,10},{10,12},{12,14},{14,16},{16,18},{18... | collective-permute-start | bytes 393224 | tf_op jit(solution)/shard_map/while/body/eval_jaxpr/ppermute | solution.py:18
  662.4 13.3 %collective-permute-start.1 = (bf16[2,4,128,64]{2,3,1,0:T(8,128)(2,1)S(1)}, bf16[2,4,128,64]{2,3,1,0:T(8,128)(2,1)S(1)}, u32[]{:S(2)}, u32[]{:S(2)}) collective-permute-start(bf16[2,4,128,64]{2,3,1,0:T(8,128)(2,1)S(1)} %copy.207), channel_id=1, source_target_pairs={{0,2},{2,4},{4,6},{6,8},{8,10},{10,12},{12,14},{14,16},{16,18},{18... | collective-permute-start | bytes 393224 | tf_op jit(solution)/shard_map/while/body/eval_jaxpr/ppermute | solution.py:18
  675.7 13.3 %collective-permute-start = (bf16[2,4,128,64]{2,3,1,0:T(8,128)(2,1)S(1)}, bf16[2,4,128,64]{2,3,1,0:T(8,128)(2,1)S(1)}, u32[]{:S(2)}, u32[]{:S(2)}) collective-permute-start(bf16[2,4,128,64]{2,3,1,0:T(8,128)(2,1)S(1)} %copy.206), channel_id=1, source_target_pairs={{0,2},{2,4},{4,6},{6,8},{8,10},{10,12},{12,14},{14,16},{16,18},{18... | collective-permute-start | bytes 393224 | tf_op jit(solution)/shard_map/while/body/eval_jaxpr/ppermute | solution.py:18
  675.8 13.2 %collective-permute-start.1 = (bf16[2,4,128,64]{2,3,1,0:T(8,128)(2,1)S(1)}, bf16[2,4,128,64]{2,3,1,0:T(8,128)(2,1)S(1)}, u32[]{:S(2)}, u32[]{:S(2)}) collective-permute-start(bf16[2,4,128,64]{2,3,1,0:T(8,128)(2,1)S(1)} %copy.207), channel_id=1, source_target_pairs={{0,2},{2,4},{4,6},{6,8},{8,10},{10,12},{12,14},{14,16},{16,18},{18... | collective-permute-start | bytes 393224 | tf_op jit(solution)/shard_map/while/body/eval_jaxpr/ppermute | solution.py:18
  689.1 13.3 %collective-permute-start = (bf16[2,4,128,64]{2,3,1,0:T(8,128)(2,1)S(1)}, bf16[2,4,128,64]{2,3,1,0:T(8,128)(2,1)S(1)}, u32[]{:S(2)}, u32[]{:S(2)}) collective-permute-start(bf16[2,4,128,64]{2,3,1,0:T(8,128)(2,1)S(1)} %copy.206), channel_id=1, source_target_pairs={{0,2},{2,4},{4,6},{6,8},{8,10},{10,12},{12,14},{14,16},{16,18},{18... | collective-permute-start | bytes 393224 | tf_op jit(solution)/shard_map/while/body/eval_jaxpr/ppermute | solution.py:18
  689.1 13.2 %collective-permute-start.1 = (bf16[2,4,128,64]{2,3,1,0:T(8,128)(2,1)S(1)}, bf16[2,4,128,64]{2,3,1,0:T(8,128)(2,1)S(1)}, u32[]{:S(2)}, u32[]{:S(2)}) collective-permute-start(bf16[2,4,128,64]{2,3,1,0:T(8,128)(2,1)S(1)} %copy.207), channel_id=1, source_target_pairs={{0,2},{2,4},{4,6},{6,8},{8,10},{10,12},{12,14},{14,16},{16,18},{18... | collective-permute-start | bytes 393224 | tf_op jit(solution)/shard_map/while/body/eval_jaxpr/ppermute | solution.py:18
  702.4 13.3 %collective-permute-start = (bf16[2,4,128,64]{2,3,1,0:T(8,128)(2,1)S(1)}, bf16[2,4,128,64]{2,3,1,0:T(8,128)(2,1)S(1)}, u32[]{:S(2)}, u32[]{:S(2)}) collective-permute-start(bf16[2,4,128,64]{2,3,1,0:T(8,128)(2,1)S(1)} %copy.206), channel_id=1, source_target_pairs={{0,2},{2,4},{4,6},{6,8},{8,10},{10,12},{12,14},{14,16},{16,18},{18... | collective-permute-start | bytes 393224 | tf_op jit(solution)/shard_map/while/body/eval_jaxpr/ppermute | solution.py:18
  702.5 13.3 %collective-permute-start.1 = (bf16[2,4,128,64]{2,3,1,0:T(8,128)(2,1)S(1)}, bf16[2,4,128,64]{2,3,1,0:T(8,128)(2,1)S(1)}, u32[]{:S(2)}, u32[]{:S(2)}) collective-permute-start(bf16[2,4,128,64]{2,3,1,0:T(8,128)(2,1)S(1)} %copy.207), channel_id=1, source_target_pairs={{0,2},{2,4},{4,6},{6,8},{8,10},{10,12},{12,14},{14,16},{16,18},{18... | collective-permute-start | bytes 393224 | tf_op jit(solution)/shard_map/while/body/eval_jaxpr/ppermute | solution.py:18
  715.8 13.3 %collective-permute-start = (bf16[2,4,128,64]{2,3,1,0:T(8,128)(2,1)S(1)}, bf16[2,4,128,64]{2,3,1,0:T(8,128)(2,1)S(1)}, u32[]{:S(2)}, u32[]{:S(2)}) collective-permute-start(bf16[2,4,128,64]{2,3,1,0:T(8,128)(2,1)S(1)} %copy.206), channel_id=1, source_target_pairs={{0,2},{2,4},{4,6},{6,8},{8,10},{10,12},{12,14},{14,16},{16,18},{18... | collective-permute-start | bytes 393224 | tf_op jit(solution)/shard_map/while/body/eval_jaxpr/ppermute | solution.py:18
  737.4 96.7 %all-reduce.20.cloned.1.call-start = ((), (), s32[]{:S(2)}) async-start(), calls=%async_computation.23 | async-start | bytes 2097152 | tf_op jit(solution)/shard_map/psum | solution.py:208
  741.8 152.0 %reduce-scatter.12.cloned.1.call-start = ((), (), s32[]{:S(2)}) async-start(), calls=%async_computation.16 | async-start | bytes 557056 | tf_op jit(solution)/shard_map/reduce_scatter | solution.py:353
  744.1 210.2 %reduce-scatter.8.cloned.1.call-start = ((), (), s32[]{:S(2)}) async-start(), calls=%async_computation.14 | async-start | bytes 1114112 | tf_op jit(solution)/shard_map/reduce_scatter | solution.py:347
  745.7 268.6 %reduce-scatter.14.cloned.1.call-start = ((), (), s32[]{:S(2)}) async-start(), calls=%async_computation.17 | async-start | bytes 1114112 | tf_op jit(solution)/shard_map/reduce_scatter | solution.py:362
  747.6 345.5 %reduce-scatter.16.cloned.1.call-start = ((), (), s32[]{:S(2)}) async-start(), calls=%async_computation.18 | async-start | bytes 5013504 | tf_op jit(solution)/shard_map/reduce_scatter | solution.py:368
  752.8 418.7 %reduce-scatter.18.cloned.1.call-start = ((), (), s32[]{:S(2)}) async-start(), calls=%async_computation.19 | async-start | bytes 5013504 | tf_op jit(solution)/shard_map/reduce_scatter | solution.py:371
  757.7 492.6 %reduce-scatter.20.cloned.1.call-start = ((), (), s32[]{:S(2)}) async-start(), calls=%async_computation.20 | async-start | bytes 5013504 | tf_op jit(solution)/shard_map/reduce_scatter | solution.py:374
  (94 other events, 1464.7 us)
Sparse Core Ops, SparseCore 0:
  10.2 40.7 all-gather.10
  93.6 47.5 all-gather.20
  143.9 47.4 all-gather.22
  193.4 37.8 all-gather.12
  269.3 28.5 all-reduce.15
  300.2 53.2 all-gather.14
  356.0 51.7 all-gather.16
  410.4 51.7 all-gather.18
  475.9 27.1 all-reduce.17
  737.5 53.6 reduce-scatter.9
  794.8 39.2 all-reduce.19
  838.1 55.7 reduce-scatter.11
  897.9 56.4 reduce-scatter.7
  957.8 56.4 reduce-scatter.13
  1018.5 74.5 reduce-scatter.15
  1096.8 74.6 reduce-scatter.17
  1175.7 74.5 reduce-scatter.19
where the time goes:
time: 1260 us
  waiting for transfers between devices  819 us (65%)
  matrix products  142 us (11%)
  blocking collectives  132 us (10%)
  local copies, waits for them, and re-layouts  83.1 us (7%)
  other arithmetic  52.8 us (4%)
  between operations  17.8 us (1%)
    ppermute x64, waiting for transfers between devices, passed_along(): lax.ppermute(shard, axis, [(i, (i + by) % devices) for i in range(devices)])  124 us
    reduce_scatter x1, waiting for transfers between devices, shards(): lax.psum_scatter(gate_wgrad.astype(jnp.bfloat16), 'ctx', scatter_dimensio...  77.3 us
    reduce_scatter x1, waiting for transfers between devices, shards(): lax.psum_scatter(down_grad.astype(jnp.bfloat16), 'ctx', scatter_dimension...  77 us
    reduce_scatter x1, waiting for transfers between devices, shards(): lax.psum_scatter(up_wgrad.astype(jnp.bfloat16), 'ctx', scatter_dimension=...  76.6 us
    unnamed x2, blocking collectives  64 us
    reduce_scatter x1, waiting for transfers between devices, shards(): lax.psum_scatter(out_wgrad.astype(jnp.bfloat16), 'ctx', scatter_dimension...  58.5 us
    all_gather x1, waiting for transfers between devices, shards(): lax.all_gather(w_gate, 'ctx', axis=0, tiled=True)  53.1 us
    reduce_scatter x1, waiting for transfers between devices, shards(): lax.psum_scatter(query_wgrad.astype(jnp.bfloat16), 'ctx', scatter_dimensi...  49.5 us
  transfers between devices with their start and end apart: 81, of which 47 were waited for; matrix products, arithmetic and copies ran while one was open for 19% of the time, Pallas kernels for 0%

commit v1 on v0

v1 whole, which is shorter than its diff:
```python
import math

import jax
import jax.numpy as jnp
from jax import lax
from jax.experimental import pallas as pl
from jax.experimental.pallas import tpu as pltpu
from jax.sharding import PartitionSpec as P

DH = 64


EPS = 1e-05
THETA = 1000000.0
SCALE = 0.125


VMEM_LIMIT = 48 * 1024 * 1024
EXTRA_ROWS = 16


def swapped(shard, axis, bit):
    devices = lax.axis_size(axis)
    return lax.ppermute(shard, axis, [(i, i ^ bit) for i in range(devices)])


def step_bits(devices):
    bits = []
    bit = devices // 2
    while bit:
        bits.append(bit)
        bit //= 2
    return bits


def slot_offsets(devices):
    offsets = [0]
    for bit in step_bits(devices):
        offsets = offsets + [item ^ bit for item in offsets]
    return offsets


def gather_slots(shard, axis):
    gathered = shard[None]
    for bit in step_bits(lax.axis_size(axis)):
        gathered = jnp.concatenate([gathered, swapped(gathered, axis, bit)], axis=0)
    return gathered


def scatter_slots(slots, axis):
    current = slots
    for bit in reversed(step_bits(lax.axis_size(axis))):
        half = current.shape[0] // 2
        arrived = swapped(current[half:], axis, bit)
        summed = current[:half].astype(jnp.float32) + arrived.astype(jnp.float32)
        current = summed.astype(jnp.bfloat16) if bit * 2 < lax.axis_size(axis) else summed
    return current[0]


def tp_sum(part):
    if lax.axis_size("tp") == 2:
        return part.astype(jnp.float32) + swapped(part, "tp", 1).astype(jnp.float32)
    return lax.psum(part, "tp").astype(jnp.float32)


def product(left, right):
    return jnp.dot(left, right, preferred_element_type=jnp.float32)


def norm_rows(values):
    factor = lax.rsqrt(jnp.mean(values * values, axis=-1, keepdims=True) + EPS)
    return (values * factor, factor)


def norm_back(gradient, normed, factor, gain):
    scaled = gradient * gain
    return factor * (scaled - normed * jnp.mean(scaled * normed, axis=-1, keepdims=True))


def rotate(values, cosine, sine_part):
    half_dim = values.shape[-1] // 2
    first_half = values[..., :half_dim]
    second_half = values[..., half_dim:]
    return jnp.concatenate(
        [
            first_half * cosine - second_half * sine_part,
            second_half * cosine + first_half * sine_part,
        ],
        axis=-1,
    )


def to_heads(flattened, sequences, key_heads, group_size):
    row_count = flattened.size // (sequences * key_heads * group_size * DH)
    arranged = flattened.reshape(sequences, row_count, key_heads, group_size, DH)
    return arranged.transpose(0, 2, 3, 1, 4).reshape(
        sequences, key_heads, group_size * row_count, DH
    )


def from_heads(stacked, group_size):
    sequences = stacked.shape[0]
    key_heads = stacked.shape[1]
    row_count = stacked.shape[2] // group_size
    arranged = stacked.reshape(sequences, key_heads, group_size, row_count, DH).transpose(
        0, 3, 1, 2, 4
    )
    return arranged.reshape(sequences * row_count, key_heads * group_size * DH)


def softmax_block(query_ref, pair_ref, query_place_ref, key_place_ref):
    pair = pair_ref[...]
    pair = pair.reshape(pair.shape[0] * pair.shape[3], pair.shape[4])
    key_rows = pair[:, :DH]
    value_rows = pair[:, DH:]
    query_rows = query_ref[0, 0] * SCALE
    scores = lax.dot_general(
        query_rows, key_rows, (((1,), (1,)), ((), ())), preferred_element_type=jnp.float32
    )
    scores = jnp.where(key_place_ref[0] <= query_place_ref[0], scores, -1e30)
    weights = jnp.exp(scores - jnp.max(scores, axis=-1, keepdims=True))
    weights = weights * (1.0 / jnp.sum(weights, axis=-1, keepdims=True))
    return query_rows, key_rows, value_rows, weights


def attend_kernel(query_ref, pair_ref, query_place_ref, key_place_ref, out_ref):
    unused_query, unused_key, value_rows, weights = softmax_block(
        query_ref, pair_ref, query_place_ref, key_place_ref
    )
    out_ref[0, 0] = product(weights.astype(jnp.bfloat16), value_rows).astype(out_ref.dtype)


def attend_back_kernel(
    query_ref, pair_ref, query_place_ref, key_place_ref, grad_ref, query_grad_ref, pair_grad_ref
):
    query_rows, key_rows, value_rows, weights = softmax_block(
        query_ref, pair_ref, query_place_ref, key_place_ref
    )
    grad_rows = grad_ref[0, 0]
    weight_grad = lax.dot_general(
        grad_rows, value_rows, (((1,), (1,)), ((), ())), preferred_element_type=jnp.float32
    )
    delta = jnp.sum(weights * weight_grad, axis=-1, keepdims=True)
    score_grad = (weights * (weight_grad - delta)).astype(jnp.bfloat16)
    query_grad_ref[0, 0] = product(score_grad, key_rows) * SCALE
    across = (((0,), (0,)), ((), ()))
    key_grad = lax.dot_general(
        score_grad, query_rows, across, preferred_element_type=jnp.float32
    )
    value_grad = lax.dot_general(
        weights.astype(jnp.bfloat16), grad_rows, across, preferred_element_type=jnp.float32
    )
    pair_grad = jnp.concatenate([key_grad, value_grad], axis=-1).astype(pair_grad_ref.dtype)
    pair_grad_ref[...] = pair_grad.reshape(pair_grad_ref.shape)


def attend_call(kernel, arrays, out_shapes, transcendentals):
    queries, pairs = arrays[0], arrays[1]
    sequences, key_heads, query_rows, unused = queries.shape
    slots, seq_rows = pairs.shape[0], pairs.shape[3]
    key_rows = slots * seq_rows

    def spec_of(array):
        if len(array.shape) == 5:
            return pl.BlockSpec((slots, 1, 1, seq_rows, 2 * DH), lambda s, h: (0, s, h, 0, 0))
        return pl.BlockSpec((1, 1, query_rows, DH), lambda s, h: (s, h, 0, 0))

    place_specs = [
        pl.BlockSpec((1, query_rows, 1), lambda s, h: (s, 0, 0)),
        pl.BlockSpec((1, 1, key_rows), lambda s, h: (s, 0, 0)),
    ]
    work = sequences * key_heads * query_rows * key_rows
    return pl.pallas_call(
        kernel,
        grid=(sequences, key_heads),
        in_specs=[spec_of(queries), spec_of(pairs)]
        + place_specs
        + [spec_of(array) for array in arrays[4:]],
        out_specs=[spec_of(shape) for shape in out_shapes],
        out_shape=out_shapes,
        compiler_params=pltpu.CompilerParams(vmem_limit_bytes=VMEM_LIMIT),
        cost_estimate=pl.CostEstimate(
            flops=4 * DH * work * transcendentals,
            bytes_accessed=4 * pairs.size,
            transcendentals=work,
        ),
    )(*arrays)


def shards(
    states,
    span_order,
    attn_gain,
    w_query,
    w_key,
    w_value,
    query_gain,
    key_gain,
    w_out,
    ffn_gain,
    w_gate,
    w_up,
    w_down,
    grad_out,
):
    ctx_count = lax.axis_size("ctx")
    own_index = lax.axis_index("ctx")
    token_rows, width = states.shape
    sequences = span_order.shape[1] // 2
    seq_rows = token_rows // sequences
    span_len = seq_rows // 2
    shard_rows = w_query.shape[0]
    query_cols = w_query.shape[1]
    key_cols = w_key.shape[1]
    query_heads = query_cols // DH
    key_heads = key_cols // DH
    group_size = query_heads // key_heads
    gain_part = query_gain.shape[0]
    attn_cols = query_cols + 2 * key_cols

    owners = own_index ^ jnp.array(slot_offsets(ctx_count), jnp.int32)
    source_column = (owners[:, None] * shard_rows + jnp.arange(shard_rows)[None, :]).reshape(width)
    to_slots = (jnp.arange(width)[:, None] == source_column[None, :]).astype(jnp.bfloat16)
    states_slots = product(states, to_slots).astype(jnp.bfloat16)
    grad_out_slots = product(grad_out, to_slots).astype(jnp.bfloat16)

    packed_cols = attn_cols + query_cols
    small = jnp.concatenate(
        [attn_gain, ffn_gain, query_gain, key_gain, span_order[0].astype(jnp.bfloat16)]
    )
    small_rows = jnp.pad(small[None, :], ((0, EXTRA_ROWS - 1), (0, packed_cols - small.shape[0])))
    packed = jnp.concatenate(
        [jnp.concatenate([w_query, w_key, w_value, w_out.T], axis=1), small_rows], axis=0
    )
    gathered = gather_slots(packed, "ctx")
    qkv_full = gathered[:, :shard_rows, :attn_cols].reshape(width, attn_cols)
    out_full = gathered[:, :shard_rows, attn_cols:].reshape(width, query_cols)
    small_full = gathered[:, shard_rows, : small.shape[0]]
    ends = [shard_rows, 2 * shard_rows, 2 * shard_rows + gain_part, 2 * shard_rows + 2 * gain_part]
    gain_attn = small_full[:, : ends[0]].reshape(width).astype(jnp.float32)
    gain_ffn = small_full[:, ends[0] : ends[1]].reshape(width).astype(jnp.float32)
    by_owner = (jnp.arange(ctx_count)[:, None] == owners[None, :]).astype(jnp.float32)
    gain_query = jnp.sum(
        by_owner[:, :, None] * small_full[None, :, ends[1] : ends[2]].astype(jnp.float32), axis=1
    ).reshape(DH)
    gain_key = jnp.sum(
        by_owner[:, :, None] * small_full[None, :, ends[2] : ends[3]].astype(jnp.float32), axis=1
    ).reshape(DH)
    order_slots = small_full[:, ends[3] :].astype(jnp.int32)
    offsets = jnp.arange(span_len, dtype=jnp.int32)
    every_place = (order_slots.reshape(ctx_count, sequences, 2, 1) * span_len + offsets).reshape(
        ctx_count, sequences, seq_rows
    )
    own_place = every_place[0]
    key_place = jnp.transpose(every_place, (1, 0, 2)).reshape(sequences, 1, ctx_count * seq_rows)
    query_place = jnp.tile(own_place, (1, group_size))[:, :, None]

    w_gate, w_up, w_down, qkv_full = lax.optimization_barrier((w_gate, w_up, w_down, qkv_full))
    gate_full = gather_slots(w_gate, "ctx").reshape(width, -1)
    up_full = gather_slots(w_up, "ctx").reshape(width, -1)
    down_full = gather_slots(w_down.T, "ctx").reshape(width, -1)

    inputs = states_slots.astype(jnp.float32)
    normed_one, factor_one = norm_rows(inputs)
    hidden_one = (normed_one * gain_attn).astype(jnp.bfloat16)
    qkv = product(hidden_one, qkv_full)
    query_pre = qkv[:, :query_cols].reshape(token_rows, query_heads, DH)
    key_pre = qkv[:, query_cols : query_cols + key_cols].reshape(token_rows, key_heads, DH)
    value_low = qkv[:, query_cols + key_cols :].astype(jnp.bfloat16)
    half_dim = DH // 2
    inverse_freq = jnp.exp(-math.log(THETA) * jnp.arange(half_dim, dtype=jnp.float32) / half_dim)
    angles = own_place.reshape(token_rows).astype(jnp.float32)[:, None] * inverse_freq[None, :]
    cosine = jnp.cos(angles)[:, None, :]
    sine_part = jnp.sin(angles)[:, None, :]
    query_normed, query_factor = norm_rows(query_pre)
    key_normed, key_factor = norm_rows(key_pre)
    query_rot = rotate(query_normed * gain_query, cosine, sine_part).astype(jnp.bfloat16)
    key_rot = rotate(key_normed * gain_key, cosine, sine_part).astype(jnp.bfloat16)
    queries = to_heads(query_rot, sequences, key_heads, group_size)
    keys = to_heads(key_rot, sequences, key_heads, 1)
    values = to_heads(value_low, sequences, key_heads, 1)
    pairs = gather_slots(jnp.concatenate([keys, values], axis=-1), "ctx")
    attend_inputs = (queries, pairs, query_place, key_place)
    (attended,) = attend_call(
        attend_kernel, attend_inputs, [jax.ShapeDtypeStruct(queries.shape, jnp.bfloat16)], 1
    )
    mixed_low = from_heads(attended, group_size)
    attn_terms = jnp.einsum("ta,da->td", mixed_low, out_full, preferred_element_type=jnp.float32)
    middle = inputs + tp_sum(attn_terms.astype(jnp.bfloat16))
    normed_two, factor_two = norm_rows(middle)
    hidden_two = (normed_two * gain_ffn).astype(jnp.bfloat16)
    gate_proj = product(hidden_two, gate_full)
    up_proj = product(hidden_two, up_full)
    sigmoid_gate = 1.0 / (1.0 + jnp.exp(-gate_proj))
    activated = gate_proj * sigmoid_gate
    inner = (activated * up_proj).astype(jnp.bfloat16)
    slotted = lambda grad: grad.astype(jnp.bfloat16).reshape(ctx_count, shard_rows, -1)
    down_grad = jnp.einsum("td,tf->df", grad_out_slots, inner, preferred_element_type=jnp.float32)
    down_share = scatter_slots(slotted(down_grad), "ctx")
    inner_grad = product(grad_out_slots, down_full)
    gate_grad = (
        inner_grad * up_proj * sigmoid_gate * (1.0 + gate_proj * (1.0 - sigmoid_gate))
    ).astype(jnp.bfloat16)
    up_grad = (inner_grad * activated).astype(jnp.bfloat16)
    hidden_two_part = jnp.einsum(
        "tf,cf->tc", gate_grad, gate_full, preferred_element_type=jnp.float32
    ) + jnp.einsum("tf,cf->tc", up_grad, up_full, preferred_element_type=jnp.float32)
    hidden_two_grad = tp_sum(hidden_two_part.astype(jnp.bfloat16))
    gate_wgrad = jnp.einsum("tc,tf->cf", hidden_two, gate_grad, preferred_element_type=jnp.float32)
    gate_share = scatter_slots(slotted(gate_wgrad), "ctx")
    up_wgrad = jnp.einsum("tc,tf->cf", hidden_two, up_grad, preferred_element_type=jnp.float32)
    up_share = scatter_slots(slotted(up_wgrad), "ctx")
    ffn_terms = jnp.einsum("tf,df->td", inner, down_full, preferred_element_type=jnp.float32)
    output_slots = (middle + tp_sum(ffn_terms.astype(jnp.bfloat16))).astype(jnp.bfloat16)
    output_low = jnp.einsum(
        "td,ed->te", output_slots, to_slots, preferred_element_type=jnp.float32
    ).astype(jnp.bfloat16)
    ffn_gain_grad = jnp.sum(hidden_two_grad * normed_two, axis=0)
    middle_grad = grad_out_slots.astype(jnp.float32) + norm_back(
        hidden_two_grad, normed_two, factor_two, gain_ffn
    )
    branch_low = middle_grad.astype(jnp.bfloat16)
    out_wgrad = jnp.einsum("td,ta->da", branch_low, mixed_low, preferred_element_type=jnp.float32)
    mixed_grad = product(branch_low, out_full).astype(jnp.bfloat16)
    attended_grad = to_heads(mixed_grad, sequences, key_heads, group_size)
    query_grad, pair_grad = attend_call(
        attend_back_kernel,
        attend_inputs + (attended_grad,),
        [
            jax.ShapeDtypeStruct(queries.shape, jnp.float32),
            jax.ShapeDtypeStruct(pairs.shape, jnp.bfloat16),
        ],
        3,
    )
    pair_share = scatter_slots(pair_grad, "ctx")
    query_rot_grad = from_heads(query_grad, group_size).reshape(token_rows, query_heads, DH)
    key_rot_grad = from_heads(pair_share[..., :DH], 1).reshape(token_rows, key_heads, DH)
    value_grad_low = from_heads(pair_share[..., DH:], 1).astype(jnp.bfloat16)
    query_out_grad = rotate(query_rot_grad, cosine, -sine_part)
    key_out_grad = rotate(key_rot_grad, cosine, -sine_part)
    query_gain_grad = jnp.sum(query_out_grad * query_normed, axis=(0, 1))
    key_gain_grad = jnp.sum(key_out_grad * key_normed, axis=(0, 1))
    query_pre_grad = norm_back(query_out_grad, query_normed, query_factor, gain_query)
    key_pre_grad = norm_back(key_out_grad, key_normed, key_factor, gain_key)
    qkv_grad = jnp.concatenate(
        [
            query_pre_grad.reshape(token_rows, query_cols).astype(jnp.bfloat16),
            key_pre_grad.reshape(token_rows, key_cols).astype(jnp.bfloat16),
            value_grad_low,
        ],
        axis=1,
    )
    hidden_one_part = jnp.einsum(
        "ta,ca->tc", qkv_grad, qkv_full, preferred_element_type=jnp.float32
    )
    gain_terms = jnp.concatenate([query_gain_grad, key_gain_grad])[None, :]
    gain_rows = jnp.pad(gain_terms, ((0, EXTRA_ROWS - 1), (0, width - gain_terms.shape[1])))
    summed = tp_sum(jnp.concatenate([hidden_one_part, gain_rows], axis=0).astype(jnp.bfloat16))
    qkv_wgrad = jnp.einsum("tc,ta->ca", hidden_one, qkv_grad, preferred_element_type=jnp.float32)
    hidden_one_grad = summed[:token_rows]
    attn_gain_grad = jnp.sum(hidden_one_grad * normed_one, axis=0)
    states_slots_grad = middle_grad + norm_back(
        hidden_one_grad, normed_one, factor_one, gain_attn
    )
    states_grad = jnp.einsum(
        "td,ed->te",
        states_slots_grad,
        to_slots.astype(jnp.float32),
        precision=lax.Precision.HIGHEST,
        preferred_element_type=jnp.float32,
    )
    gain_sums = summed[token_rows, : 2 * DH].reshape(2, ctx_count, gain_part)
    gain_slots = jnp.sum(by_owner[None, :, :, None] * gain_sums[:, :, None, :], axis=1)
    small_grads = jnp.concatenate(
        [
            attn_gain_grad.reshape(ctx_count, shard_rows),
            ffn_gain_grad.reshape(ctx_count, shard_rows),
            gain_slots[0],
            gain_slots[1],
        ],
        axis=1,
    ).astype(jnp.bfloat16)
    small_share = scatter_slots(small_grads[:, None, :], "ctx")[0]
    attn_share = scatter_slots(
        slotted(jnp.concatenate([qkv_wgrad, out_wgrad], axis=1)), "ctx"
    )
    return (
        output_low,
        states_grad,
        small_share[: ends[0]],
        attn_share[:, :query_cols],
        attn_share[:, query_cols : query_cols + key_cols],
        attn_share[:, query_cols + key_cols : attn_cols],
        small_share[ends[1] : ends[2]],
        small_share[ends[2] : ends[3]],
        attn_share[:, attn_cols:].T,
        small_share[ends[0] : ends[1]],
        gate_share,
        up_share,
        down_share.T,
    )


def solution(mesh):
    in_specs = (
        P("ctx", None),
        P("ctx", None),
        P("ctx"),
        P("ctx", "tp"),
        P("ctx", "tp"),
        P("ctx", "tp"),
        P("ctx"),
        P("ctx"),
        P("tp", "ctx"),
        P("ctx"),
        P("ctx", "tp"),
        P("ctx", "tp"),
        P("tp", "ctx"),
        P("ctx", None),
    )
    out_specs = (
        P("ctx", None),
        P("ctx", None),
        P("ctx"),
        P("ctx", "tp"),
        P("ctx", "tp"),
        P("ctx", "tp"),
        P("ctx"),
        P("ctx"),
        P("tp", "ctx"),
        P("ctx"),
        P("ctx", "tp"),
        P("ctx", "tp"),
        P("tp", "ctx"),
    )
    return jax.shard_map(shards, mesh=mesh, in_specs=in_specs, out_specs=out_specs, check_vma=False)
```

time: 1260 us -> 603 us (0.48)
  waiting for transfers between devices: 819 us -> 337 us
  blocking collectives: 132 us -> 0 us
  matrix products: 142 us -> 47.5 us
  starting transfers between devices: 9.68 us -> 45.6 us
  Pallas kernels: 0 us -> 31.1 us
  between operations: 17.8 us -> 2.64 us
    reduce_scatter x7 -> x0, waiting for transfers between devices: 390 us -> none  [the longest x1 77.3 us: shards(): lax.psum_scatter(gate_wgrad.astype(jnp.bfloat16), 'ctx', scatter_dimensio...]
    all_gather x7 -> x0, waiting for transfers between devices: 215 us -> none  [the longest x1 53.1 us: shards(): lax.all_gather(w_gate, 'ctx', axis=0, tiled=True)]
    ppermute x64 -> x48, waiting for transfers between devices: 124 us -> 337 us  [swapped(): return lax.ppermute(shard, axis, [(i, i ^ bit) for i in range(devices)])]
    psum x3 -> x0, waiting for transfers between devices: 86.3 us -> none  [the longest x1 41.5 us: shards(): lax.psum(ffn_terms.astype(jnp.bfloat16), 'tp').astype(jnp.float32)]
    dot_general x124 -> x10, matrix products: 112 us -> 35 us  [the longest x1 13.7 us: shards(): jnp.einsum('tf,cf->tc', gate_grad, gate_full, preferred_element_type=jnp....]
    unnamed x2 -> x0, blocking collectives: 64 us -> none
    all_gather x3 -> x0, blocking collectives: 62.7 us -> none  [the longest x1 23.1 us: shards(): order_table = lax.all_gather(span_order, 'ctx', axis=0, tiled=True)]
    ppermute x64 -> x48, starting transfers between devices: 8.33 us -> 45.6 us  [swapped(): return lax.ppermute(shard, axis, [(i, i ^ bit) for i in range(devices)])]
  transfers between devices with their start and end apart: 81 -> 48, of which waited for: 47 -> 28; matrix products, arithmetic and copies ran while one was open for 19% -> 24% of each run, Pallas kernels for 0% -> 5%
where the time goes in v1:
time: 603 us; the launch traced here: 593 us
  waiting for transfers between devices  337 us (56%)
  local copies, waits for them, and re-layouts  77.5 us (13%)
  other arithmetic  51.8 us (9%)
  matrix products  47.5 us (8%)
  starting transfers between devices  45.6 us (8%)
  Pallas kernels  31.1 us (5%)
    ppermute x48, waiting for transfers between devices, swapped(): return lax.ppermute(shard, axis, [(i, i ^ bit) for i in range(devices)])  337 us
    ppermute x48, starting transfers between devices, swapped(): return lax.ppermute(shard, axis, [(i, i ^ bit) for i in range(devices)])  45.6 us
    pallas_call x2, Pallas kernels, attend_call(): pl.pallas_call(kernel, grid=(sequences, key_heads), in_specs=[spec_of(que...  31.1 us
    unnamed x161, local copies, waits for them, and re-layouts  19 us
    concatenate x15, other arithmetic, gather_slots(): gathered = jnp.concatenate([gathered, swapped(gathered, axis, bit)], axis=0)  18.3 us
    convert_element_type x18, other arithmetic, scatter_slots(): summed.astype(jnp.bfloat16)  14.4 us
    slice x24, local copies, waits for them, and re-layouts, scatter_slots(): arrived = swapped(current[half:], axis, bit)  13.7 us
    dot_general x1, matrix products, shards(): jnp.einsum('tf,cf->tc', gate_grad, gate_full, preferred_element_type=jnp....  13.7 us
  transfers between devices with their start and end apart: 48, of which 28 were waited for; matrix products, arithmetic and copies ran while one was open for 24% of the time, Pallas kernels for 5%

profile of v1, /device:TPU:0, one launch (start us, length us, event | category | flops | bytes accessed | tf_op | source)
XLA Modules:
  0.0 593.2 jit_solution(8704116785336539119)
XLA Ops:
  1.4 2.8 concatenate.141
  5.1 4.1 collective-permute-start
  9.2 11.2 %collective-permute-done = bf16[1,80,1536]{2,1,0:T(8,128)(2,1)S(1)} collective-permute-done((bf16[1,80,1536]{2,1,0:T(8,128)(2,1)S(1)}, bf16[1,80,1536]{2,1,0:T(8,128)(2,1)S(1)}, u32[]{:S(2)}, u32[]{:S(2)}) %collective-permute-start) | collective-permute-done | bytes 245792 | tf_op jit(solution)/shard_map/ppermute | solution.py:24
  21.3 11.7 %collective-permute-done.1 = bf16[2,80,1536]{2,1,0:T(8,128)(2,1)S(1)} collective-permute-done((bf16[2,80,1536]{2,1,0:T(8,128)(2,1)S(1)}, bf16[2,80,1536]{2,1,0:T(8,128)(2,1)S(1)}, u32[]{:S(2)}, u32[]{:S(2)}) %collective-permute-start.1) | collective-permute-done | bytes 491552 | tf_op jit(solution)/shard_map/ppermute | solution.py:24
  35.3 20.9 %collective-permute-done.2 = bf16[4,80,1536]{2,1,0:T(8,128)(2,1)S(1)} collective-permute-done((bf16[4,80,1536]{2,1,0:T(8,128)(2,1)}, bf16[4,80,1536]{2,1,0:T(8,128)(2,1)S(1)}, u32[]{:S(2)}, u32[]{:S(2)}) %collective-permute-start.2) | collective-permute-done | bytes 983072 | tf_op jit(solution)/shard_map/ppermute | solution.py:24
  75.8 4.2 collective-permute-start.4
  86.8 2.9 collective-permute-start.13
  96.5 15.5 %collective-permute-done.4 = bf16[1,2,4,128,128]{4,3,2,1,0:T(8,128)(2,1)} collective-permute-done((bf16[1,2,4,128,128]{4,3,2,1,0:T(8,128)(2,1)}, bf16[1,2,4,128,128]{4,3,2,1,0:T(8,128)(2,1)}, u32[]{:S(2)}, u32[]{:S(2)}) %collective-permute-start.4) | collective-permute-done | bytes 262176 | tf_op jit(solution)/shard_map/ppermute | solution.py:24
  115.1 3.3 collective-permute-done.17
  119.6 5.0 collective-permute-done.13
  126.1 4.4 collective-permute-done.9
  135.5 6.2 %collective-permute-done.5 = bf16[2,2,4,128,128]{4,3,2,1,0:T(8,128)(2,1)S(1)} collective-permute-done((bf16[2,2,4,128,128]{4,3,2,1,0:T(8,128)(2,1)S(1)}, bf16[2,2,4,128,128]{4,3,2,1,0:T(8,128)(2,1)S(1)}, u32[]{:S(2)}, u32[]{:S(2)}) %collective-permute-start.5) | collective-permute-done | bytes 524320 | tf_op jit(solution)/shard_map/ppermute | solution.py:24
  144.5 9.8 %collective-permute-done.18 = bf16[2,64,2304]{2,1,0:T(8,128)(2,1)S(1)} collective-permute-done((bf16[2,64,2304]{2,1,0:T(8,128)(2,1)S(1)}, bf16[2,64,2304]{2,1,0:T(8,128)(2,1)S(1)}, u32[]{:S(2)}, u32[]{:S(2)}) %collective-permute-start.18) | collective-permute-done | bytes 589856 | tf_op jit(solution)/shard_map/ppermute | solution.py:24
  156.9 10.0 %collective-permute-done.14 = bf16[2,64,2304]{2,1,0:T(8,128)(2,1)S(1)} collective-permute-done((bf16[2,64,2304]{2,1,0:T(8,128)(2,1)S(1)}, bf16[2,64,2304]{2,1,0:T(8,128)(2,1)S(1)}, u32[]{:S(2)}, u32[]{:S(2)}) %collective-permute-start.14) | collective-permute-done | bytes 589856 | tf_op jit(solution)/shard_map/ppermute | solution.py:24
  169.6 9.9 %collective-permute-done.10 = bf16[2,64,2304]{2,1,0:T(8,128)(2,1)S(1)} collective-permute-done((bf16[2,64,2304]{2,1,0:T(8,128)(2,1)S(1)}, bf16[2,64,2304]{2,1,0:T(8,128)(2,1)S(1)}, u32[]{:S(2)}, u32[]{:S(2)}) %collective-permute-start.10) | collective-permute-done | bytes 589856 | tf_op jit(solution)/shard_map/ppermute | solution.py:24
  185.3 8.9 %collective-permute-done.19 = bf16[4,64,2304]{2,1,0:T(8,128)(2,1)S(1)} collective-permute-done((bf16[4,64,2304]{2,1,0:T(8,128)(2,1)S(1)}, bf16[4,64,2304]{2,1,0:T(8,128)(2,1)S(1)}, u32[]{:S(2)}, u32[]{:S(2)}) %collective-permute-start.19) | collective-permute-done | bytes 1179680 | tf_op jit(solution)/shard_map/ppermute | solution.py:24
  194.2 2.6 pad_maximum_fusion.2
  196.8 22.7 %collective-permute-done.15 = bf16[4,64,2304]{2,1,0:T(8,128)(2,1)S(1)} collective-permute-done((bf16[4,64,2304]{2,1,0:T(8,128)(2,1)S(1)}, bf16[4,64,2304]{2,1,0:T(8,128)(2,1)S(1)}, u32[]{:S(2)}, u32[]{:S(2)}) %collective-permute-start.15) | collective-permute-done | bytes 1179680 | tf_op jit(solution)/shard_map/ppermute | solution.py:24
  219.5 2.6 pad_maximum_fusion.1
  222.1 21.6 %collective-permute-done.11 = bf16[4,64,2304]{2,1,0:T(8,128)(2,1)S(1)} collective-permute-done((bf16[4,64,2304]{2,1,0:T(8,128)(2,1)S(1)}, bf16[4,64,2304]{2,1,0:T(8,128)(2,1)S(1)}, u32[]{:S(2)}, u32[]{:S(2)}) %collective-permute-start.11) | collective-permute-done | bytes 1179680 | tf_op jit(solution)/shard_map/ppermute | solution.py:24
  249.0 11.1 %shard_map.246 = bf16[2,4,256,64]{3,2,1,0:T(8,128)(2,1)S(1)} custom-call(bf16[2,4,256,64]{3,2,1,0:T(8,128)(2,1)S(1)} %bitcast.176, bf16[16,2,4,128,128]{4,3,2,1,0:T(8,128)(2,1)S(1)} %constant_dynamic-update-slice_fusion.5.pair_ref, s32[2,256,1]{2,1,0:T(8,128)S(1)} %tile.12.query_place_ref, s32[2,1,2048]{2,1,0:T(1,128)S(1)} %bitcast.180), custom_call_target="tpu_custom_call" | custom-call | flops 1073741824 | bytes 8388608 | tf_op jit(solution)/shard_map/pallas_call | solution.py:173
  263.7 3.2 constant_dynamic-update-slice_fusion.20
  267.0 3.3 constant_dynamic-update-slice_fusion.15
  290.3 13.7 %fusion.31 = bf16[256,1024]{0,1:T(8,128)(2,1)S(1)} fusion(f32[256,1024]{0,1:T(8,128)S(1)} %fusion.67, bf16[256,2304]{1,0:T(8,128)(2,1)S(1)} %get-tuple-element.41, bf16[1024,2304]{1,0:T(8,128)(2,1)S(1)} %bitcast.223), kind=kOutput, calls=%fused_computation.55 | convolution fusion | flops 1208483840 | bytes 7471104 | tf_op jit(solution)/shard_map/tf,cf->tc/dot_general | solution.py:305
  310.1 2.5 fusion.60
  312.6 4.8 collective-permute-done.22
  320.3 20.1 %shard_map.247 = (f32[2,4,256,64]{3,2,1,0:T(8,128)S(1)}, bf16[16,2,4,128,128]{4,3,2,1,0:T(8,128)(2,1)}) custom-call(bf16[2,4,256,64]{3,2,1,0:T(8,128)(2,1)S(1)} %bitcast.177, bf16[16,2,4,128,128]{4,3,2,1,0:T(8,128)(2,1)} %copy-done.3, s32[2,256,1]{2,1,0:T(8,128)S(1)} %tile.12.query_place_ref, s32[2,1,2048]{2,1,0:T(1,128)S(1)} %bitcast.181, ...), custom_call_target="tpu_custom_call" | custom-call | flops 3221225472 | bytes 8388608 | tf_op jit(solution)/shard_map/pallas_call | solution.py:173
  340.4 3.2 slice.302
  348.8 2.7 convolution_convert_fusion.4
  351.6 3.4 fusion.24
  366.7 2.7 add_convert_fusion
  370.1 16.0 %collective-permute-done.37 = bf16[4,64,2304]{2,1,0:T(8,128)(2,1)S(1)} collective-permute-done((bf16[4,64,2304]{2,1,0:T(8,128)(2,1)S(1)}, bf16[4,64,2304]{2,1,0:T(8,128)(2,1)S(1)}, u32[]{:S(2)}, u32[]{:S(2)}) %collective-permute-start.37) | collective-permute-done | bytes 1179680 | tf_op jit(solution)/shard_map/ppermute | solution.py:24
  386.5 24.9 %collective-permute-done.41 = bf16[4,64,2304]{2,1,0:T(8,128)(2,1)S(1)} collective-permute-done((bf16[4,64,2304]{2,1,0:T(8,128)(2,1)S(1)}, bf16[4,64,2304]{2,1,0:T(8,128)(2,1)S(1)}, u32[]{:S(2)}, u32[]{:S(2)}) %collective-permute-start.41) | collective-permute-done | bytes 1179680 | tf_op jit(solution)/shard_map/ppermute | solution.py:24
  411.8 24.9 %collective-permute-done.45 = bf16[4,64,2304]{2,1,0:T(8,128)(2,1)S(1)} collective-permute-done((bf16[4,64,2304]{2,1,0:T(8,128)(2,1)S(1)}, bf16[4,64,2304]{2,1,0:T(8,128)(2,1)S(1)}, u32[]{:S(2)}, u32[]{:S(2)}) %collective-permute-start.45) | collective-permute-done | bytes 1179680 | tf_op jit(solution)/shard_map/ppermute | solution.py:24
  437.1 21.5 %collective-permute-done.24 = bf16[4,2,4,128,128]{4,3,2,1,0:T(8,128)(2,1)S(1)} collective-permute-done((bf16[4,2,4,128,128]{4,3,2,1,0:T(8,128)(2,1)S(1)}, bf16[4,2,4,128,128]{4,3,2,1,0:T(8,128)(2,1)S(1)}, u32[]{:S(2)}, u32[]{:S(2)}) %collective-permute-start.24) | collective-permute-done | bytes 1048608 | tf_op jit(solution)/shard_map/ppermute | solution.py:24
  459.3 4.1 collective-permute-start.39
  464.6 2.9 collective-permute-start.47
  467.5 15.7 %collective-permute-done.25 = bf16[2,2,4,128,128]{4,3,2,1,0:T(8,128)(2,1)S(1)} collective-permute-done((bf16[2,2,4,128,128]{4,3,2,1,0:T(8,128)(2,1)S(1)}, bf16[2,2,4,128,128]{4,3,2,1,0:T(8,128)(2,1)S(1)}, u32[]{:S(2)}, u32[]{:S(2)}) %collective-permute-start.25) | collective-permute-done | bytes 524320 | tf_op jit(solution)/shard_map/ppermute | solution.py:24
  484.4 17.8 %collective-permute-done.43 = bf16[1,64,2304]{2,1,0:T(8,128)(2,1)S(1)} collective-permute-done((bf16[1,64,2304]{2,1,0:T(8,128)(2,1)S(1)}, bf16[1,64,2304]{2,1,0:T(8,128)(2,1)S(1)}, u32[]{:S(2)}, u32[]{:S(2)}) %collective-permute-start.43) | collective-permute-done | bytes 294944 | tf_op jit(solution)/shard_map/ppermute | solution.py:24
  503.1 9.6 %collective-permute-done.26 = bf16[1,2,4,128,128]{4,3,2,1,0:T(8,128)(2,1)S(1)} collective-permute-done((bf16[1,2,4,128,128]{4,3,2,1,0:T(8,128)(2,1)S(1)}, bf16[1,2,4,128,128]{4,3,2,1,0:T(8,128)(2,1)S(1)}, u32[]{:S(2)}, u32[]{:S(2)}) %collective-permute-start.26) | collective-permute-done | bytes 262176 | tf_op jit(solution)/shard_map/ppermute | solution.py:24
  527.2 8.2 %collective-permute-done.27 = bf16[272,1024]{1,0:T(8,128)(2,1)} collective-permute-done((bf16[272,1024]{1,0:T(8,128)(2,1)}, bf16[272,1024]{1,0:T(8,128)(2,1)}, u32[]{:S(2)}, u32[]{:S(2)}) %collective-permute-start.27) | collective-permute-done | bytes 557088 | tf_op jit(solution)/shard_map/ppermute | solution.py:24
  542.1 3.7 copy.246
  547.4 2.9 add_convert_fusion.1
  551.1 4.9 fusion.3
  556.0 3.0 collective-permute-start.31
  559.0 11.1 %collective-permute-done.33 = bf16[4,64,1536]{2,1,0:T(8,128)(2,1)S(1)} collective-permute-done((bf16[4,64,1536]{2,1,0:T(8,128)(2,1)S(1)}, bf16[4,64,1536]{2,1,0:T(8,128)(2,1)S(1)}, u32[]{:S(2)}, u32[]{:S(2)}) %collective-permute-start.33) | collective-permute-done | bytes 786464 | tf_op jit(solution)/shard_map/ppermute | solution.py:24
  571.0 9.8 %collective-permute-done.34 = bf16[2,64,1536]{2,1,0:T(8,128)(2,1)S(1)} collective-permute-done((bf16[2,64,1536]{2,1,0:T(8,128)(2,1)S(1)}, bf16[2,64,1536]{2,1,0:T(8,128)(2,1)S(1)}, u32[]{:S(2)}, u32[]{:S(2)}) %collective-permute-start.34) | collective-permute-done | bytes 393248 | tf_op jit(solution)/shard_map/ppermute | solution.py:24
  582.8 8.6 %collective-permute-done.35 = bf16[1,64,1536]{2,1,0:T(8,128)(2,1)S(1)} collective-permute-done((bf16[1,64,1536]{2,1,0:T(8,128)(2,1)S(1)}, bf16[1,64,1536]{2,1,0:T(8,128)(2,1)S(1)}, u32[]{:S(2)}, u32[]{:S(2)}) %collective-permute-start.35) | collective-permute-done | bytes 196640 | tf_op jit(solution)/shard_map/ppermute | solution.py:24
  (432 shorter events, 150.0 us)
Async XLA Ops:
  5.1 15.3 %collective-permute-start = (bf16[1,80,1536]{2,1,0:T(8,128)(2,1)S(1)}, bf16[1,80,1536]{2,1,0:T(8,128)(2,1)S(1)}, u32[]{:S(2)}, u32[]{:S(2)}) collective-permute-start(bf16[1,80,1536]{2,1,0:T(8,128)(2,1)S(1)} %fusion.49), channel_id=1, source_target_pairs={{0,16},{2,18},{4,20},{6,22},{8,24},{10,26},{12,28},{14,30},{16,0},... | collective-permute-start | bytes 737288 | tf_op jit(solution)/shard_map/ppermute | solution.py:24
  20.5 12.5 %collective-permute-start.1 = (bf16[2,80,1536]{2,1,0:T(8,128)(2,1)S(1)}, bf16[2,80,1536]{2,1,0:T(8,128)(2,1)S(1)}, u32[]{:S(2)}, u32[]{:S(2)}) collective-permute-start(bf16[2,80,1536]{2,1,0:T(8,128)(2,1)S(1)} %pad_maximum_fusion.17), channel_id=1, source_target_pairs={{0,8},{2,10},{4,12},{6,14},{8,0},{10,2},{12,4},{14,6},{16,24},{18,... | collective-permute-start | bytes 1474568 | tf_op jit(solution)/shard_map/ppermute | solution.py:24
  34.0 22.2 %collective-permute-start.2 = (bf16[4,80,1536]{2,1,0:T(8,128)(2,1)}, bf16[4,80,1536]{2,1,0:T(8,128)(2,1)S(1)}, u32[]{:S(2)}, u32[]{:S(2)}) collective-permute-start(bf16[4,80,1536]{2,1,0:T(8,128)(2,1)} %pad_maximum_fusion.10), channel_id=1, source_target_pairs={{0,4},{2,6},{4,0},{6,2},{8,12},{10,14},{12,8},{14,10},{16,20},{18,... | collective-permute-start | bytes 2949128 | tf_op jit(solution)/shard_map/ppermute | solution.py:24
  57.8 4.3 collective-permute-start.3
  75.8 36.2 %collective-permute-start.4 = (bf16[1,2,4,128,128]{4,3,2,1,0:T(8,128)(2,1)}, bf16[1,2,4,128,128]{4,3,2,1,0:T(8,128)(2,1)}, u32[]{:S(2)}, u32[]{:S(2)}) collective-permute-start(bf16[1,2,4,128,128]{4,3,2,1,0:T(8,128)(2,1)} %get-tuple-element.34), channel_id=1, source_target_pairs={{0,16},{2,18},{4,20},{6,22},{8,24},{10,26},{12,28},{14,30},{16,0},... | collective-permute-start | bytes 786440 | tf_op jit(solution)/shard_map/ppermute | solution.py:24
  86.1 32.3 %collective-permute-start.17 = (bf16[1,64,2304]{2,1,0:T(8,128)(2,1)S(1)}, bf16[1,64,2304]{2,1,0:T(8,128)(2,1)}, u32[]{:S(2)}, u32[]{:S(2)}) collective-permute-start(bf16[1,64,2304]{2,1,0:T(8,128)(2,1)S(1)} %bitcast.194), channel_id=1, source_target_pairs={{0,16},{2,18},{4,20},{6,22},{8,24},{10,26},{12,28},{14,30},{16,0},... | collective-permute-start | bytes 884744 | tf_op jit(solution)/shard_map/ppermute | solution.py:24
  86.8 37.8 %collective-permute-start.13 = (bf16[1,64,2304]{2,1,0:T(8,128)(2,1)}, bf16[1,64,2304]{2,1,0:T(8,128)(2,1)S(1)}, u32[]{:S(2)}, u32[]{:S(2)}) collective-permute-start(bf16[1,64,2304]{2,1,0:T(8,128)(2,1)} %bitcast.22), channel_id=1, source_target_pairs={{0,16},{2,18},{4,20},{6,22},{8,24},{10,26},{12,28},{14,30},{16,0},... | collective-permute-start | bytes 884744 | tf_op jit(solution)/shard_map/ppermute | solution.py:24
  89.7 40.7 %collective-permute-start.9 = (bf16[1,64,2304]{2,1,0:T(8,128)(2,1)}, bf16[1,64,2304]{2,1,0:T(8,128)(2,1)S(1)}, u32[]{:S(2)}, u32[]{:S(2)}) collective-permute-start(bf16[1,64,2304]{2,1,0:T(8,128)(2,1)} %bitcast.198), channel_id=1, source_target_pairs={{0,16},{2,18},{4,20},{6,22},{8,24},{10,26},{12,28},{14,30},{16,0},... | collective-permute-start | bytes 884744 | tf_op jit(solution)/shard_map/ppermute | solution.py:24
  113.0 28.6 %collective-permute-start.5 = (bf16[2,2,4,128,128]{4,3,2,1,0:T(8,128)(2,1)S(1)}, bf16[2,2,4,128,128]{4,3,2,1,0:T(8,128)(2,1)S(1)}, u32[]{:S(2)}, u32[]{:S(2)}) collective-permute-start(bf16[2,2,4,128,128]{4,3,2,1,0:T(8,128)(2,1)S(1)} %pad_maximum_fusion.14), channel_id=1, source_target_pairs={{0,8},{2,10},{4,12},{6,14},{8,0},{10,2},{12,4},{14,6},{16,24},{18,... | collective-permute-start | bytes 1572872 | tf_op jit(solution)/shard_map/ppermute | solution.py:24
  119.4 34.9 %collective-permute-start.18 = (bf16[2,64,2304]{2,1,0:T(8,128)(2,1)S(1)}, bf16[2,64,2304]{2,1,0:T(8,128)(2,1)S(1)}, u32[]{:S(2)}, u32[]{:S(2)}) collective-permute-start(bf16[2,64,2304]{2,1,0:T(8,128)(2,1)S(1)} %pad_maximum_fusion.13), channel_id=1, source_target_pairs={{0,8},{2,10},{4,12},{6,14},{8,0},{10,2},{12,4},{14,6},{16,24},{18,... | collective-permute-start | bytes 1769480 | tf_op jit(solution)/shard_map/ppermute | solution.py:24
  125.6 41.3 %collective-permute-start.14 = (bf16[2,64,2304]{2,1,0:T(8,128)(2,1)S(1)}, bf16[2,64,2304]{2,1,0:T(8,128)(2,1)S(1)}, u32[]{:S(2)}, u32[]{:S(2)}) collective-permute-start(bf16[2,64,2304]{2,1,0:T(8,128)(2,1)S(1)} %pad_maximum_fusion.12), channel_id=1, source_target_pairs={{0,8},{2,10},{4,12},{6,14},{8,0},{10,2},{12,4},{14,6},{16,24},{18,... | collective-permute-start | bytes 1769480 | tf_op jit(solution)/shard_map/ppermute | solution.py:24
  131.5 48.0 %collective-permute-start.10 = (bf16[2,64,2304]{2,1,0:T(8,128)(2,1)S(1)}, bf16[2,64,2304]{2,1,0:T(8,128)(2,1)S(1)}, u32[]{:S(2)}, u32[]{:S(2)}) collective-permute-start(bf16[2,64,2304]{2,1,0:T(8,128)(2,1)S(1)} %pad_maximum_fusion.11), channel_id=1, source_target_pairs={{0,8},{2,10},{4,12},{6,14},{8,0},{10,2},{12,4},{14,6},{16,24},{18,... | collective-permute-start | bytes 1769480 | tf_op jit(solution)/shard_map/ppermute | solution.py:24
  142.8 41.0 %collective-permute-start.6 = (bf16[4,2,4,128,128]{4,3,2,1,0:T(8,128)(2,1)S(1)}, bf16[4,2,4,128,128]{4,3,2,1,0:T(8,128)(2,1)S(1)}, u32[]{:S(2)}, u32[]{:S(2)}) collective-permute-start(bf16[4,2,4,128,128]{4,3,2,1,0:T(8,128)(2,1)S(1)} %pad_maximum_fusion.9), channel_id=1, source_target_pairs={{0,4},{2,6},{4,0},{6,2},{8,12},{10,14},{12,8},{14,10},{16,20},{18,... | collective-permute-start | bytes 3145736 | tf_op jit(solution)/shard_map/ppermute | solution.py:24
  155.4 38.8 %collective-permute-start.19 = (bf16[4,64,2304]{2,1,0:T(8,128)(2,1)S(1)}, bf16[4,64,2304]{2,1,0:T(8,128)(2,1)S(1)}, u32[]{:S(2)}, u32[]{:S(2)}) collective-permute-start(bf16[4,64,2304]{2,1,0:T(8,128)(2,1)S(1)} %pad_maximum_fusion.8), channel_id=1, source_target_pairs={{0,4},{2,6},{4,0},{6,2},{8,12},{10,14},{12,8},{14,10},{16,20},{18,... | collective-permute-start | bytes 3538952 | tf_op jit(solution)/shard_map/ppermute | solution.py:24
  168.0 51.4 %collective-permute-start.15 = (bf16[4,64,2304]{2,1,0:T(8,128)(2,1)S(1)}, bf16[4,64,2304]{2,1,0:T(8,128)(2,1)S(1)}, u32[]{:S(2)}, u32[]{:S(2)}) collective-permute-start(bf16[4,64,2304]{2,1,0:T(8,128)(2,1)S(1)} %pad_maximum_fusion.7), channel_id=1, source_target_pairs={{0,4},{2,6},{4,0},{6,2},{8,12},{10,14},{12,8},{14,10},{16,20},{18,... | collective-permute-start | bytes 3538952 | tf_op jit(solution)/shard_map/ppermute | solution.py:24
  179.6 64.1 %collective-permute-start.11 = (bf16[4,64,2304]{2,1,0:T(8,128)(2,1)S(1)}, bf16[4,64,2304]{2,1,0:T(8,128)(2,1)S(1)}, u32[]{:S(2)}, u32[]{:S(2)}) collective-permute-start(bf16[4,64,2304]{2,1,0:T(8,128)(2,1)S(1)} %pad_maximum_fusion.6), channel_id=1, source_target_pairs={{0,4},{2,6},{4,0},{6,2},{8,12},{10,14},{12,8},{14,10},{16,20},{18,... | collective-permute-start | bytes 3538952 | tf_op jit(solution)/shard_map/ppermute | solution.py:24
  185.0 63.6 %collective-permute-start.7 = (bf16[8,2,4,128,128]{4,3,2,1,0:T(8,128)(2,1)S(1)}, bf16[8,2,4,128,128]{4,3,2,1,0:T(8,128)(2,1)S(1)}, u32[]{:S(2)}, u32[]{:S(2)}) collective-permute-start(bf16[8,2,4,128,128]{4,3,2,1,0:T(8,128)(2,1)S(1)} %pad_maximum_fusion.3), channel_id=1, source_target_pairs={{0,2},{2,0},{4,6},{6,4},{8,10},{10,8},{12,14},{14,12},{16,18},{18,... | collective-permute-start | bytes 6291464 | tf_op jit(solution)/shard_map/ppermute | solution.py:24
  196.8 66.9 %collective-permute-start.20 = (bf16[8,64,2304]{2,1,0:T(8,128)(2,1)}, bf16[8,64,2304]{2,1,0:T(8,128)(2,1)}, u32[]{:S(2)}, u32[]{:S(2)}) collective-permute-start(bf16[8,64,2304]{2,1,0:T(8,128)(2,1)} %pad_maximum_fusion.2), channel_id=1, source_target_pairs={{0,2},{2,0},{4,6},{6,4},{8,10},{10,8},{12,14},{14,12},{16,18},{18,... | collective-permute-start | bytes 7077896 | tf_op jit(solution)/shard_map/ppermute | solution.py:24
  222.1 44.9 %collective-permute-start.16 = (bf16[8,64,2304]{2,1,0:T(8,128)(2,1)}, bf16[8,64,2304]{2,1,0:T(8,128)(2,1)}, u32[]{:S(2)}, u32[]{:S(2)}) collective-permute-start(bf16[8,64,2304]{2,1,0:T(8,128)(2,1)} %pad_maximum_fusion.1), channel_id=1, source_target_pairs={{0,2},{2,0},{4,6},{6,4},{8,10},{10,8},{12,14},{14,12},{16,18},{18,... | collective-permute-start | bytes 7077896 | tf_op jit(solution)/shard_map/ppermute | solution.py:24
  245.3 24.9 %collective-permute-start.12 = (bf16[8,64,2304]{2,1,0:T(8,128)(2,1)}, bf16[8,64,2304]{2,1,0:T(8,128)(2,1)}, u32[]{:S(2)}, u32[]{:S(2)}) collective-permute-start(bf16[8,64,2304]{2,1,0:T(8,128)(2,1)} %pad_maximum_fusion), channel_id=1, source_target_pairs={{0,2},{2,0},{4,6},{6,4},{8,10},{10,8},{12,14},{14,12},{16,18},{18,... | collective-permute-start | bytes 7077896 | tf_op jit(solution)/shard_map/ppermute | solution.py:24
  262.1 14.4 %collective-permute-start.8 = (bf16[256,1024]{0,1:T(8,128)(2,1)S(1)}, bf16[256,1024]{0,1:T(8,128)(2,1)S(1)}, u32[]{:S(2)}, u32[]{:S(2)}) collective-permute-start(bf16[256,1024]{0,1:T(8,128)(2,1)S(1)} %convolution_convert_fusion.5), channel_id=1, source_target_pairs={{0,1},{1,0},{2,3},{3,2},{4,5},{5,4},{6,7},{7,6},{8,9},{9,8},{10,11... | collective-permute-start | bytes 1572872 | tf_op jit(solution)/shard_map/ppermute | solution.py:24
  287.4 64.2 %collective-permute-start.21 = (bf16[256,1024]{0,1:T(8,128)(2,1)}, bf16[256,1024]{0,1:T(8,128)(2,1)}, u32[]{:S(2)}, u32[]{:S(2)}) collective-permute-start(bf16[256,1024]{0,1:T(8,128)(2,1)} %convolution_convert_fusion.6), channel_id=1, source_target_pairs={{0,1},{1,0},{2,3},{3,2},{4,5},{5,4},{6,7},{7,6},{8,9},{9,8},{10,11... | collective-permute-start | bytes 1572872 | tf_op jit(solution)/shard_map/ppermute | solution.py:24
  304.1 13.3 %collective-permute-start.22 = (bf16[256,1024]{0,1:T(8,128)(2,1)S(1)}, bf16[256,1024]{0,1:T(8,128)(2,1)S(1)}, u32[]{:S(2)}, u32[]{:S(2)}) collective-permute-start(bf16[256,1024]{0,1:T(8,128)(2,1)S(1)} %fusion.31), channel_id=1, source_target_pairs={{0,1},{1,0},{2,3},{3,2},{4,5},{5,4},{6,7},{7,6},{8,9},{9,8},{10,11... | collective-permute-start | bytes 1572872 | tf_op jit(solution)/shard_map/ppermute | solution.py:24
  307.0 47.9 %collective-permute-start.36 = (bf16[8,64,2304]{2,1,0:T(8,128)(2,1)}, bf16[8,64,2304]{2,1,0:T(8,128)(2,1)}, u32[]{:S(2)}, u32[]{:S(2)}) collective-permute-start(bf16[8,64,2304]{2,1,0:T(8,128)(2,1)} %bitcast.59), channel_id=1, source_target_pairs={{0,2},{2,0},{4,6},{6,4},{8,10},{10,8},{12,14},{14,12},{16,18},{18,... | collective-permute-start | bytes 7077896 | tf_op jit(solution)/shard_map/ppermute | solution.py:24
  309.6 49.3 %collective-permute-start.40 = (bf16[8,64,2304]{2,1,0:T(8,128)(2,1)}, bf16[8,64,2304]{2,1,0:T(8,128)(2,1)}, u32[]{:S(2)}, u32[]{:S(2)}) collective-permute-start(bf16[8,64,2304]{2,1,0:T(8,128)(2,1)} %bitcast.62), channel_id=1, source_target_pairs={{0,2},{2,0},{4,6},{6,4},{8,10},{10,8},{12,14},{14,12},{16,18},{18,... | collective-permute-start | bytes 7077896 | tf_op jit(solution)/shard_map/ppermute | solution.py:24
  312.6 50.1 %collective-permute-start.44 = (bf16[8,64,2304]{2,1,0:T(8,128)(2,1)}, bf16[8,64,2304]{2,1,0:T(8,128)(2,1)}, u32[]{:S(2)}, u32[]{:S(2)}) collective-permute-start(bf16[8,64,2304]{2,1,0:T(8,128)(2,1)} %bitcast.65), channel_id=1, source_target_pairs={{0,2},{2,0},{4,6},{6,4},{8,10},{10,8},{12,14},{14,12},{16,18},{18,... | collective-permute-start | bytes 7077896 | tf_op jit(solution)/shard_map/ppermute | solution.py:24
  343.6 23.1 %collective-permute-start.23 = (bf16[8,2,4,128,128]{4,3,2,1,0:T(8,128)(2,1)}, bf16[8,2,4,128,128]{4,3,2,1,0:T(8,128)(2,1)}, u32[]{:S(2)}, u32[]{:S(2)}) collective-permute-start(bf16[8,2,4,128,128]{4,3,2,1,0:T(8,128)(2,1)} %slice.302), channel_id=1, source_target_pairs={{0,2},{2,0},{4,6},{6,4},{8,10},{10,8},{12,14},{14,12},{16,18},{18,... | collective-permute-start | bytes 6291464 | tf_op jit(solution)/shard_map/ppermute | solution.py:24
  357.3 28.9 %collective-permute-start.37 = (bf16[4,64,2304]{2,1,0:T(8,128)(2,1)S(1)}, bf16[4,64,2304]{2,1,0:T(8,128)(2,1)S(1)}, u32[]{:S(2)}, u32[]{:S(2)}) collective-permute-start(bf16[4,64,2304]{2,1,0:T(8,128)(2,1)S(1)} %slice.433), channel_id=1, source_target_pairs={{0,4},{2,6},{4,0},{6,2},{8,12},{10,14},{12,8},{14,10},{16,20},{18,... | collective-permute-start | bytes 3538952 | tf_op jit(solution)/shard_map/ppermute | solution.py:24
  361.1 50.3 %collective-permute-start.41 = (bf16[4,64,2304]{2,1,0:T(8,128)(2,1)S(1)}, bf16[4,64,2304]{2,1,0:T(8,128)(2,1)S(1)}, u32[]{:S(2)}, u32[]{:S(2)}) collective-permute-start(bf16[4,64,2304]{2,1,0:T(8,128)(2,1)S(1)} %slice.441), channel_id=1, source_target_pairs={{0,4},{2,6},{4,0},{6,2},{8,12},{10,14},{12,8},{14,10},{16,20},{18,... | collective-permute-start | bytes 3538952 | tf_op jit(solution)/shard_map/ppermute | solution.py:24
  365.2 71.5 %collective-permute-start.45 = (bf16[4,64,2304]{2,1,0:T(8,128)(2,1)S(1)}, bf16[4,64,2304]{2,1,0:T(8,128)(2,1)S(1)}, u32[]{:S(2)}, u32[]{:S(2)}) collective-permute-start(bf16[4,64,2304]{2,1,0:T(8,128)(2,1)S(1)} %slice.449), channel_id=1, source_target_pairs={{0,4},{2,6},{4,0},{6,2},{8,12},{10,14},{12,8},{14,10},{16,20},{18,... | collective-permute-start | bytes 3538952 | tf_op jit(solution)/shard_map/ppermute | solution.py:24
  369.5 89.1 %collective-permute-start.24 = (bf16[4,2,4,128,128]{4,3,2,1,0:T(8,128)(2,1)S(1)}, bf16[4,2,4,128,128]{4,3,2,1,0:T(8,128)(2,1)S(1)}, u32[]{:S(2)}, u32[]{:S(2)}) collective-permute-start(bf16[4,2,4,128,128]{4,3,2,1,0:T(8,128)(2,1)S(1)} %slice.393), channel_id=1, source_target_pairs={{0,4},{2,6},{4,0},{6,2},{8,12},{10,14},{12,8},{14,10},{16,20},{18,... | collective-permute-start | bytes 3145736 | tf_op jit(solution)/shard_map/ppermute | solution.py:24
  386.4 72.7 %collective-permute-start.38 = (bf16[2,64,2304]{2,1,0:T(8,128)(2,1)S(1)}, bf16[2,64,2304]{2,1,0:T(8,128)(2,1)S(1)}, u32[]{:S(2)}, u32[]{:S(2)}) collective-permute-start(bf16[2,64,2304]{2,1,0:T(8,128)(2,1)S(1)} %slice.435), channel_id=1, source_target_pairs={{0,8},{2,10},{4,12},{6,14},{8,0},{10,2},{12,4},{14,6},{16,24},{18,... | collective-permute-start | bytes 1769480 | tf_op jit(solution)/shard_map/ppermute | solution.py:24
  411.7 51.7 %collective-permute-start.42 = (bf16[2,64,2304]{2,1,0:T(8,128)(2,1)S(1)}, bf16[2,64,2304]{2,1,0:T(8,128)(2,1)S(1)}, u32[]{:S(2)}, u32[]{:S(2)}) collective-permute-start(bf16[2,64,2304]{2,1,0:T(8,128)(2,1)S(1)} %slice.443), channel_id=1, source_target_pairs={{0,8},{2,10},{4,12},{6,14},{8,0},{10,2},{12,4},{14,6},{16,24},{18,... | collective-permute-start | bytes 1769480 | tf_op jit(solution)/shard_map/ppermute | solution.py:24
  437.0 26.7 %collective-permute-start.46 = (bf16[2,64,2304]{2,1,0:T(8,128)(2,1)S(1)}, bf16[2,64,2304]{2,1,0:T(8,128)(2,1)S(1)}, u32[]{:S(2)}, u32[]{:S(2)}) collective-permute-start(bf16[2,64,2304]{2,1,0:T(8,128)(2,1)S(1)} %slice.451), channel_id=1, source_target_pairs={{0,8},{2,10},{4,12},{6,14},{8,0},{10,2},{12,4},{14,6},{16,24},{18,... | collective-permute-start | bytes 1769480 | tf_op jit(solution)/shard_map/ppermute | solution.py:24
  459.0 24.2 %collective-permute-start.25 = (bf16[2,2,4,128,128]{4,3,2,1,0:T(8,128)(2,1)S(1)}, bf16[2,2,4,128,128]{4,3,2,1,0:T(8,128)(2,1)S(1)}, u32[]{:S(2)}, u32[]{:S(2)}) collective-permute-start(bf16[2,2,4,128,128]{4,3,2,1,0:T(8,128)(2,1)S(1)} %slice.395), channel_id=1, source_target_pairs={{0,8},{2,10},{4,12},{6,14},{8,0},{10,2},{12,4},{14,6},{16,24},{18,... | collective-permute-start | bytes 1572872 | tf_op jit(solution)/shard_map/ppermute | solution.py:24
  459.3 24.2 %collective-permute-start.39 = (bf16[1,64,2304]{2,1,0:T(8,128)(2,1)S(1)}, bf16[1,64,2304]{2,1,0:T(8,128)(2,1)S(1)}, u32[]{:S(2)}, u32[]{:S(2)}) collective-permute-start(bf16[1,64,2304]{2,1,0:T(8,128)(2,1)S(1)} %slice.437), channel_id=1, source_target_pairs={{0,16},{2,18},{4,20},{6,22},{8,24},{10,26},{12,28},{14,30},{16,0},... | collective-permute-start | bytes 884744 | tf_op jit(solution)/shard_map/ppermute | solution.py:24
  463.6 38.6 %collective-permute-start.43 = (bf16[1,64,2304]{2,1,0:T(8,128)(2,1)S(1)}, bf16[1,64,2304]{2,1,0:T(8,128)(2,1)S(1)}, u32[]{:S(2)}, u32[]{:S(2)}) collective-permute-start(bf16[1,64,2304]{2,1,0:T(8,128)(2,1)S(1)} %slice.445), channel_id=1, source_target_pairs={{0,16},{2,18},{4,20},{6,22},{8,24},{10,26},{12,28},{14,30},{16,0},... | collective-permute-start | bytes 884744 | tf_op jit(solution)/shard_map/ppermute | solution.py:24
  464.6 75.6 %collective-permute-start.47 = (bf16[1,64,2304]{2,1,0:T(8,128)(2,1)}, bf16[1,64,2304]{2,1,0:T(8,128)(2,1)}, u32[]{:S(2)}, u32[]{:S(2)}) collective-permute-start(bf16[1,64,2304]{2,1,0:T(8,128)(2,1)} %slice.453), channel_id=1, source_target_pairs={{0,16},{2,18},{4,20},{6,22},{8,24},{10,26},{12,28},{14,30},{16,0},... | collective-permute-start | bytes 884744 | tf_op jit(solution)/shard_map/ppermute | solution.py:24
  483.4 29.3 %collective-permute-start.26 = (bf16[1,2,4,128,128]{4,3,2,1,0:T(8,128)(2,1)S(1)}, bf16[1,2,4,128,128]{4,3,2,1,0:T(8,128)(2,1)S(1)}, u32[]{:S(2)}, u32[]{:S(2)}) collective-permute-start(bf16[1,2,4,128,128]{4,3,2,1,0:T(8,128)(2,1)S(1)} %slice.397), channel_id=1, source_target_pairs={{0,16},{2,18},{4,20},{6,22},{8,24},{10,26},{12,28},{14,30},{16,0},... | collective-permute-start | bytes 786440 | tf_op jit(solution)/shard_map/ppermute | solution.py:24
  521.9 13.5 %collective-permute-start.27 = (bf16[272,1024]{1,0:T(8,128)(2,1)}, bf16[272,1024]{1,0:T(8,128)(2,1)}, u32[]{:S(2)}, u32[]{:S(2)}) collective-permute-start(bf16[272,1024]{1,0:T(8,128)(2,1)} %copy.241), channel_id=1, source_target_pairs={{0,1},{1,0},{2,3},{3,2},{4,5},{5,4},{6,7},{7,6},{8,9},{9,8},{10,11... | collective-permute-start | bytes 1671176 | tf_op jit(solution)/shard_map/ppermute | solution.py:24
  527.2 20.2 %collective-permute-start.32 = (bf16[8,64,1536]{2,1,0:T(8,128)(2,1)}, bf16[8,64,1536]{2,1,0:T(8,128)(2,1)}, u32[]{:S(2)}, u32[]{:S(2)}) collective-permute-start(bf16[8,64,1536]{2,1,0:T(8,128)(2,1)} %bitcast.208), channel_id=1, source_target_pairs={{0,2},{2,0},{4,6},{6,4},{8,10},{10,8},{12,14},{14,12},{16,18},{18,... | collective-permute-start | bytes 4718600 | tf_op jit(solution)/shard_map/ppermute | solution.py:24
  540.2 5.6 collective-permute-start.28
  545.8 5.1 collective-permute-start.29
  550.4 19.7 %collective-permute-start.33 = (bf16[4,64,1536]{2,1,0:T(8,128)(2,1)S(1)}, bf16[4,64,1536]{2,1,0:T(8,128)(2,1)S(1)}, u32[]{:S(2)}, u32[]{:S(2)}) collective-permute-start(bf16[4,64,1536]{2,1,0:T(8,128)(2,1)S(1)} %slice.418), channel_id=1, source_target_pairs={{0,4},{2,6},{4,0},{6,2},{8,12},{10,14},{12,8},{14,10},{16,20},{18,... | collective-permute-start | bytes 2359304 | tf_op jit(solution)/shard_map/ppermute | solution.py:24
  551.0 5.0 collective-permute-start.30
  556.0 14.4 %collective-permute-start.31 = (bf16[1,1,136]{2,0,1:T(2,128)(2,1)S(1)}, bf16[1,1,136]{2,0,1:T(2,128)(2,1)S(1)}, u32[]{:S(2)}, u32[]{:S(2)}) collective-permute-start(bf16[1,1,136]{2,0,1:T(2,128)(2,1)S(1)} %slice.413), channel_id=1, source_target_pairs={{0,16},{2,18},{4,20},{6,22},{8,24},{10,26},{12,28},{14,30},{16,0},... | collective-permute-start | bytes 824 | tf_op jit(solution)/shard_map/ppermute | solution.py:24
  570.3 10.5 %collective-permute-start.34 = (bf16[2,64,1536]{2,1,0:T(8,128)(2,1)S(1)}, bf16[2,64,1536]{2,1,0:T(8,128)(2,1)S(1)}, u32[]{:S(2)}, u32[]{:S(2)}) collective-permute-start(bf16[2,64,1536]{2,1,0:T(8,128)(2,1)S(1)} %slice.420), channel_id=1, source_target_pairs={{0,8},{2,10},{4,12},{6,14},{8,0},{10,2},{12,4},{14,6},{16,24},{18,... | collective-permute-start | bytes 1179656 | tf_op jit(solution)/shard_map/ppermute | solution.py:24
  580.9 10.5 %collective-permute-start.35 = (bf16[1,64,1536]{2,1,0:T(8,128)(2,1)S(1)}, bf16[1,64,1536]{2,1,0:T(8,128)(2,1)S(1)}, u32[]{:S(2)}, u32[]{:S(2)}) collective-permute-start(bf16[1,64,1536]{2,1,0:T(8,128)(2,1)S(1)} %slice.422), channel_id=1, source_target_pairs={{0,16},{2,18},{4,20},{6,22},{8,24},{10,26},{12,28},{14,30},{16,0},... | collective-permute-start | bytes 589832 | tf_op jit(solution)/shard_map/ppermute | solution.py:24
  (71 other events, 563.7 us)

commit v2 on v1

--- a/solution.py
+++ b/solution.py
@@ -40,21 +40,42 @@
     return offsets
 
 
-def gather_slots(shard, axis):
+def after(value, *earlier):
+    return lax.optimization_barrier((value,) + earlier)[0]
+
+
+def gather_step(gathered, axis, bit):
+    return jnp.concatenate([gathered, swapped(gathered, axis, bit)], axis=0)
+
+
+def gather_outer(shard, axis):
     gathered = shard[None]
-    for bit in step_bits(lax.axis_size(axis)):
-        gathered = jnp.concatenate([gathered, swapped(gathered, axis, bit)], axis=0)
+    for bit in step_bits(lax.axis_size(axis))[:-2]:
+        gathered = gather_step(gathered, axis, bit)
     return gathered
 
 
-def scatter_slots(slots, axis):
+def halves_of(slots):
+    half = slots.shape[0] // 2
+    return slots[:half], slots[half:]
+
+
+def added(kept, arrived):
+    return (kept.astype(jnp.float32) + arrived.astype(jnp.float32)).astype(jnp.bfloat16)
+
+
+def scatter_core(slots, axis):
+    kept, sent = halves_of(slots)
+    return added(kept, swapped(sent, axis, 1))
+
+
+def scatter_outer(slots, axis):
     current = slots
-    for bit in reversed(step_bits(lax.axis_size(axis))):
-        half = current.shape[0] // 2
-        arrived = swapped(current[half:], axis, bit)
-        summed = current[:half].astype(jnp.float32) + arrived.astype(jnp.float32)
-        current = summed.astype(jnp.bfloat16) if bit * 2 < lax.axis_size(axis) else summed
-    return current[0]
+    for bit in reversed(step_bits(lax.axis_size(axis))[:-2]):
+        kept, sent = halves_of(current)
+        arrived = swapped(sent, axis, bit)
+        current = added(kept, arrived)
+    return kept[0].astype(jnp.float32) + arrived[0].astype(jnp.float32)
 
 
 def tp_sum(part):
@@ -232,7 +253,12 @@
     packed = jnp.concatenate(
         [jnp.concatenate([w_query, w_key, w_value, w_out.T], axis=1), small_rows], axis=0
     )
-    gathered = gather_slots(packed, "ctx")
+    packed_outer = gather_outer(packed, "ctx")
+    gate_outer = gather_outer(after(w_gate, packed_outer), "ctx")
+    up_outer = gather_outer(after(w_up, gate_outer), "ctx")
+    packed_inner = gather_step(packed_outer, "ctx", 2)
+    gathered = gather_step(packed_inner, "ctx", 1)
+    gate_inner = gather_step(after(gate_outer, packed_inner), "ctx", 2)
     qkv_full = gathered[:, :shard_rows, :attn_cols].reshape(width, attn_cols)
     out_full = gathered[:, :shard_rows, attn_cols:].reshape(width, query_cols)
     small_full = gathered[:, shard_rows, : small.shape[0]]
@@ -254,11 +280,6 @@
     own_place = every_place[0]
     key_place = jnp.transpose(every_place, (1, 0, 2)).reshape(sequences, 1, ctx_count * seq_rows)
     query_place = jnp.tile(own_place, (1, group_size))[:, :, None]
-
-    w_gate, w_up, w_down, qkv_full = lax.optimization_barrier((w_gate, w_up, w_down, qkv_full))
-    gate_full = gather_slots(w_gate, "ctx").reshape(width, -1)
-    up_full = gather_slots(w_up, "ctx").reshape(width, -1)
-    down_full = gather_slots(w_down.T, "ctx").reshape(width, -1)
 
     inputs = states_slots.astype(jnp.float32)
     normed_one, factor_one = norm_rows(inputs)
@@ -279,15 +300,27 @@
     queries = to_heads(query_rot, sequences, key_heads, group_size)
     keys = to_heads(key_rot, sequences, key_heads, 1)
     values = to_heads(value_low, sequences, key_heads, 1)
-    pairs = gather_slots(jnp.concatenate([keys, values], axis=-1), "ctx")
+    pairs_outer = gather_outer(jnp.concatenate([keys, values], axis=-1), "ctx")
+    pairs_inner = gather_step(after(pairs_outer, gate_inner), "ctx", 2)
+    pairs = gather_step(pairs_inner, "ctx", 1)
+    up_sent = after(up_outer, pairs_inner)
+    up_arrived = swapped(up_sent, "ctx", 2)
+    down_outer = gather_outer(after(w_down.T, pairs_outer), "ctx")
+    down_sent = after(down_outer, up_arrived)
+    down_arrived = swapped(down_sent, "ctx", 2)
     attend_inputs = (queries, pairs, query_place, key_place)
     (attended,) = attend_call(
         attend_kernel, attend_inputs, [jax.ShapeDtypeStruct(queries.shape, jnp.bfloat16)], 1
     )
+    gate_full = gather_step(after(gate_inner, attended), "ctx", 1).reshape(width, -1)
+    up_inner = jnp.concatenate([up_sent, after(up_arrived, attended)], axis=0)
+    up_full = gather_step(up_inner, "ctx", 1).reshape(width, -1)
     mixed_low = from_heads(attended, group_size)
     attn_terms = jnp.einsum("ta,da->td", mixed_low, out_full, preferred_element_type=jnp.float32)
     middle = inputs + tp_sum(attn_terms.astype(jnp.bfloat16))
     normed_two, factor_two = norm_rows(middle)
+    down_inner = jnp.concatenate([down_sent, after(down_arrived, normed_two)], axis=0)
+    down_full = gather_step(down_inner, "ctx", 1).reshape(width, -1)
     hidden_two = (normed_two * gain_ffn).astype(jnp.bfloat16)
     gate_proj = product(hidden_two, gate_full)
     up_proj = product(hidden_two, up_full)
@@ -296,20 +329,22 @@
     inner = (activated * up_proj).astype(jnp.bfloat16)
     slotted = lambda grad: grad.astype(jnp.bfloat16).reshape(ctx_count, shard_rows, -1)
     down_grad = jnp.einsum("td,tf->df", grad_out_slots, inner, preferred_element_type=jnp.float32)
-    down_share = scatter_slots(slotted(down_grad), "ctx")
+    down_kept, down_sent = halves_of(scatter_core(slotted(down_grad), "ctx"))
+    down_arrived = swapped(down_sent, "ctx", 2)
     inner_grad = product(grad_out_slots, down_full)
     gate_grad = (
         inner_grad * up_proj * sigmoid_gate * (1.0 + gate_proj * (1.0 - sigmoid_gate))
     ).astype(jnp.bfloat16)
     up_grad = (inner_grad * activated).astype(jnp.bfloat16)
     hidden_two_part = jnp.einsum(
-        "tf,cf->tc", gate_grad, gate_full, preferred_element_type=jnp.float32
+        "tf,cf->tc", after(gate_grad, down_sent), gate_full, preferred_element_type=jnp.float32
     ) + jnp.einsum("tf,cf->tc", up_grad, up_full, preferred_element_type=jnp.float32)
     hidden_two_grad = tp_sum(hidden_two_part.astype(jnp.bfloat16))
     gate_wgrad = jnp.einsum("tc,tf->cf", hidden_two, gate_grad, preferred_element_type=jnp.float32)
-    gate_share = scatter_slots(slotted(gate_wgrad), "ctx")
+    gate_kept, gate_sent = halves_of(scatter_core(slotted(gate_wgrad), "ctx"))
+    gate_arrived = swapped(after(gate_sent, down_arrived), "ctx", 2)
     up_wgrad = jnp.einsum("tc,tf->cf", hidden_two, up_grad, preferred_element_type=jnp.float32)
-    up_share = scatter_slots(slotted(up_wgrad), "ctx")
+    up_kept, up_sent = halves_of(scatter_core(slotted(up_wgrad), "ctx"))
     ffn_terms = jnp.einsum("tf,df->td", inner, down_full, preferred_element_type=jnp.float32)
     output_slots = (middle + tp_sum(ffn_terms.astype(jnp.bfloat16))).astype(jnp.bfloat16)
     output_low = jnp.einsum(
@@ -322,7 +357,8 @@
     branch_low = middle_grad.astype(jnp.bfloat16)
     out_wgrad = jnp.einsum("td,ta->da", branch_low, mixed_low, preferred_element_type=jnp.float32)
     mixed_grad = product(branch_low, out_full).astype(jnp.bfloat16)
-    attended_grad = to_heads(mixed_grad, sequences, key_heads, group_size)
+    down_share = scatter_outer(added(down_kept, after(down_arrived, middle_grad)), "ctx")
+    attended_grad = to_heads(after(mixed_grad, gate_sent, down_arrived), sequences, key_heads, group_size)
     query_grad, pair_grad = attend_call(
         attend_back_kernel,
         attend_inputs + (attended_grad,),
@@ -332,7 +368,11 @@
         ],
         3,
     )
-    pair_share = scatter_slots(pair_grad, "ctx")
+    gate_share = scatter_outer(added(gate_kept, after(gate_arrived, pair_grad)), "ctx")
+    pair_kept, pair_sent = halves_of(scatter_core(after(pair_grad, gate_arrived), "ctx"))
+    pair_arrived = swapped(pair_sent, "ctx", 2)
+    pair_share = scatter_outer(added(pair_kept, pair_arrived), "ctx")
+    up_arrived = swapped(after(up_sent, gate_arrived, pair_arrived), "ctx", 2)
     query_rot_grad = from_heads(query_grad, group_size).reshape(token_rows, query_heads, DH)
     key_rot_grad = from_heads(pair_share[..., :DH], 1).reshape(token_rows, key_heads, DH)
     value_grad_low = from_heads(pair_share[..., DH:], 1).astype(jnp.bfloat16)
@@ -350,6 +390,7 @@
         ],
         axis=1,
     )
+    qkv_grad = after(qkv_grad, up_arrived)
     hidden_one_part = jnp.einsum(
         "ta,ca->tc", qkv_grad, qkv_full, preferred_element_type=jnp.float32
     )
@@ -380,10 +421,19 @@
         ],
         axis=1,
     ).astype(jnp.bfloat16)
-    small_share = scatter_slots(small_grads[:, None, :], "ctx")[0]
-    attn_share = scatter_slots(
-        slotted(jnp.concatenate([qkv_wgrad, out_wgrad], axis=1)), "ctx"
-    )
+    small_rows = jnp.pad(
+        small_grads[:, None, :],
+        ((0, 0), (0, EXTRA_ROWS - 1), (0, packed_cols - small_grads.shape[1])),
+    )
+    packed_grad = jnp.concatenate(
+        [slotted(jnp.concatenate([qkv_wgrad, out_wgrad], axis=1)), small_rows], axis=1
+    )
+    packed_kept, packed_sent = halves_of(scatter_core(packed_grad, "ctx"))
+    packed_arrived = swapped(after(packed_sent, up_arrived), "ctx", 2)
+    up_share = scatter_outer(added(up_kept, after(up_arrived, qkv_grad)), "ctx")
+    packed_share = scatter_outer(added(packed_kept, packed_arrived), "ctx")
+    attn_share = packed_share[:shard_rows]
+    small_share = packed_share[shard_rows]
     return (
         output_low,
         states_grad,

time: 603 us -> 546 us (0.905)
  waiting for transfers between devices: 337 us -> 283 us
  matrix products: 47.5 us -> 33.8 us
  other arithmetic: 51.8 us -> 61.3 us
    ppermute x48 -> x44, waiting for transfers between devices: 337 us -> 283 us  [swapped(): return lax.ppermute(shard, axis, [(i, i ^ bit) for i in range(devices)])]
    dot_general x1, matrix products: 13.7 us -> 1.42 us  [shards(): jnp.einsum('tf,cf->tc', after(gate_grad, down_sent), gate_full, preferred...]
    concatenate x8, local copies, waits for them, and re-layouts: 1.76 us -> 8.6 us  [rotate(): jnp.concatenate([first_half * cosine - second_half * sine_part, second_ha...]
    unnamed x161 -> x154, local copies, waits for them, and re-layouts: 19 us -> 12.4 us
    convert_element_type x19 -> x17, other arithmetic: 15.1 us -> 19.1 us  [the longest x15 17.7 us: added(): (kept.astype(jnp.float32) + arrived.astype(jnp.float32)).astype(jnp.bfloa...]
    concatenate x16 -> x18, other arithmetic: 20.4 us -> 22.6 us  [the longest x14 15.9 us: gather_step(): return jnp.concatenate([gathered, swapped(gathered, axis, bit)], axis=0)]
    ppermute x48 -> x44, starting transfers between devices: 45.6 us -> 47.5 us  [swapped(): return lax.ppermute(shard, axis, [(i, i ^ bit) for i in range(devices)])]
    slice x24 -> x20, local copies, waits for them, and re-layouts: 13.7 us -> 13.6 us  [halves_of(): return (slots[:half], slots[half:])]
  transfers between devices with their start and end apart: 48 -> 44, of which waited for: 28 -> 23; matrix products, arithmetic and copies ran while one was open for 24% -> 27% of each run, Pallas kernels for 5% -> 6%
where the time goes in v2:
time: 546 us; the launch traced here: 538 us
  waiting for transfers between devices  283 us (52%)
  local copies, waits for them, and re-layouts  77.6 us (14%)
  other arithmetic  61.3 us (11%)
  starting transfers between devices  47.5 us (9%)
  matrix products  33.8 us (6%)
  Pallas kernels  32.2 us (6%)
    ppermute x44, waiting for transfers between devices, swapped(): return lax.ppermute(shard, axis, [(i, i ^ bit) for i in range(devices)])  283 us
    ppermute x44, starting transfers between devices, swapped(): return lax.ppermute(shard, axis, [(i, i ^ bit) for i in range(devices)])  47.5 us
    pallas_call x2, Pallas kernels, attend_call(): pl.pallas_call(kernel, grid=(sequences, key_heads), in_specs=[spec_of(que...  32.2 us
    convert_element_type x15, other arithmetic, added(): (kept.astype(jnp.float32) + arrived.astype(jnp.float32)).astype(jnp.bfloa...  17.7 us
    concatenate x14, other arithmetic, gather_step(): return jnp.concatenate([gathered, swapped(gathered, axis, bit)], axis=0)  15.9 us
    slice x20, local copies, waits for them, and re-layouts, halves_of(): return (slots[:half], slots[half:])  13.6 us
    unnamed x154, local copies, waits for them, and re-layouts  12.4 us
  transfers between devices with their start and end apart: 44, of which 23 were waited for; matrix products, arithmetic and copies ran while one was open for 27% of the time, Pallas kernels for 6%

profile of v2, /device:TPU:0, one launch (start us, length us, event | category | flops | bytes accessed | tf_op | source)
XLA Modules:
  0.0 537.7 jit_solution(6870016237622025639)
XLA Ops:
  1.5 2.8 concatenate.157
  5.2 4.1 collective-permute-start
  9.3 11.2 %collective-permute-done = bf16[1,80,1536]{2,1,0:T(8,128)(2,1)S(1)} collective-permute-done((bf16[1,80,1536]{2,1,0:T(8,128)(2,1)S(1)}, bf16[1,80,1536]{2,1,0:T(8,128)(2,1)S(1)}, u32[]{:S(2)}, u32[]{:S(2)}) %collective-permute-start) | collective-permute-done | bytes 245792 | tf_op jit(solution)/shard_map/ppermute | solution.py:24
  21.3 11.7 %collective-permute-done.1 = bf16[2,80,1536]{2,1,0:T(8,128)(2,1)S(1)} collective-permute-done((bf16[2,80,1536]{2,1,0:T(8,128)(2,1)S(1)}, bf16[2,80,1536]{2,1,0:T(8,128)(2,1)S(1)}, u32[]{:S(2)}, u32[]{:S(2)}) %collective-permute-start.1) | collective-permute-done | bytes 491552 | tf_op jit(solution)/shard_map/ppermute | solution.py:24
  36.5 3.3 collective-permute-start.6
  39.8 16.5 %collective-permute-done.2 = bf16[4,80,1536]{2,1,0:T(8,128)(2,1)S(1)} collective-permute-done((bf16[4,80,1536]{2,1,0:T(8,128)(2,1)}, bf16[4,80,1536]{2,1,0:T(8,128)(2,1)S(1)}, u32[]{:S(2)}, u32[]{:S(2)}) %collective-permute-start.2) | collective-permute-done | bytes 983072 | tf_op jit(solution)/shard_map/ppermute | solution.py:24
  56.7 2.3 collective-permute-start.7
  59.1 13.9 %collective-permute-done.7 = bf16[2,64,2304]{2,1,0:T(8,128)(2,1)S(1)} collective-permute-done((bf16[2,64,2304]{2,1,0:T(8,128)(2,1)S(1)}, bf16[2,64,2304]{2,1,0:T(8,128)(2,1)S(1)}, u32[]{:S(2)}, u32[]{:S(2)}) %collective-permute-start.7) | collective-permute-done | bytes 589856 | tf_op jit(solution)/shard_map/ppermute | solution.py:24
  96.8 3.8 collective-permute-start.4
  100.6 18.7 %collective-permute-done.4 = bf16[1,2,4,128,128]{4,3,2,1,0:T(8,128)(2,1)S(1)} collective-permute-done((bf16[1,2,4,128,128]{4,3,2,1,0:T(8,128)(2,1)S(1)}, bf16[1,2,4,128,128]{4,3,2,1,0:T(8,128)(2,1)S(1)}, u32[]{:S(2)}, u32[]{:S(2)}) %collective-permute-start.4) | collective-permute-done | bytes 262176 | tf_op jit(solution)/shard_map/ppermute | solution.py:24
  119.5 2.4 constant_dynamic-update-slice_fusion.6
  121.9 2.4 constant_dynamic-update-slice_fusion.5
  124.3 11.7 %collective-permute-done.5 = bf16[2,2,4,128,128]{4,3,2,1,0:T(8,128)(2,1)S(1)} collective-permute-done((bf16[2,2,4,128,128]{4,3,2,1,0:T(8,128)(2,1)S(1)}, bf16[2,2,4,128,128]{4,3,2,1,0:T(8,128)(2,1)S(1)}, u32[]{:S(2)}, u32[]{:S(2)}) %collective-permute-start.5) | collective-permute-done | bytes 524320 | tf_op jit(solution)/shard_map/ppermute | solution.py:24
  140.0 21.3 %collective-permute-done.9 = bf16[4,2,4,128,128]{4,3,2,1,0:T(8,128)(2,1)} collective-permute-done((bf16[4,2,4,128,128]{4,3,2,1,0:T(8,128)(2,1)S(1)}, bf16[4,2,4,128,128]{4,3,2,1,0:T(8,128)(2,1)}, u32[]{:S(2)}, u32[]{:S(2)}) %collective-permute-start.9) | collective-permute-done | bytes 1048608 | tf_op jit(solution)/shard_map/ppermute | solution.py:24
  161.3 3.2 constant_dynamic-update-slice_fusion.7
  171.9 14.9 %collective-permute-done.17 = bf16[1,64,2304]{2,1,0:T(8,128)(2,1)S(1)} collective-permute-done((bf16[1,64,2304]{2,1,0:T(8,128)(2,1)S(1)}, bf16[1,64,2304]{2,1,0:T(8,128)(2,1)S(1)}, u32[]{:S(2)}, u32[]{:S(2)}) %collective-permute-start.17) | collective-permute-done | bytes 294944 | tf_op jit(solution)/shard_map/ppermute | solution.py:24
  192.7 10.2 %collective-permute-done.18 = bf16[2,64,2304]{2,1,0:T(8,128)(2,1)} collective-permute-done((bf16[2,64,2304]{2,1,0:T(8,128)(2,1)}, bf16[2,64,2304]{2,1,0:T(8,128)(2,1)}, u32[]{:S(2)}, u32[]{:S(2)}) %collective-permute-start.18) | collective-permute-done | bytes 589856 | tf_op jit(solution)/shard_map/ppermute | solution.py:24
  205.1 10.4 %collective-permute-done.15 = bf16[4,64,2304]{2,1,0:T(8,128)(2,1)} collective-permute-done((bf16[4,64,2304]{2,1,0:T(8,128)(2,1)}, bf16[4,64,2304]{2,1,0:T(8,128)(2,1)}, u32[]{:S(2)}, u32[]{:S(2)}) %collective-permute-start.15) | collective-permute-done | bytes 1179680 | tf_op jit(solution)/shard_map/ppermute | solution.py:24
  216.1 3.2 constant_dynamic-update-slice_fusion.9.pair_ref
  219.3 11.9 %shard_map.246 = bf16[2,4,256,64]{3,2,1,0:T(8,128)(2,1)S(1)} custom-call(bf16[2,4,256,64]{3,2,1,0:T(8,128)(2,1)S(1)} %bitcast.174, bf16[16,2,4,128,128]{4,3,2,1,0:T(8,128)(2,1)} %constant_dynamic-update-slice_fusion.9.pair_ref, s32[2,256,1]{2,1,0:T(8,128)S(1)} %tile.12.query_place_ref, s32[2,1,2048]{2,1,0:T(1,128)S(1)} %bitcast.178), custom_call_target="tpu_custom_call" | custom-call | flops 1073741824 | bytes 8388608 | tf_op jit(solution)/shard_map/pallas_call | solution.py:194
  235.3 3.3 pad_maximum_fusion.3
  239.2 6.9 %collective-permute-done.11 = bf16[256,1024]{0,1:T(8,128)(2,1)S(1)} collective-permute-done((bf16[256,1024]{0,1:T(8,128)(2,1)S(1)}, bf16[256,1024]{0,1:T(8,128)(2,1)S(1)}, u32[]{:S(2)}, u32[]{:S(2)}) %collective-permute-start.11) | collective-permute-done | bytes 524320 | tf_op jit(solution)/shard_map/ppermute | solution.py:24
  249.7 2.6 pad_maximum_fusion.1
  255.8 2.4 pad_maximum_fusion.2
  260.4 3.5 multiply_convert_fusion.1
  270.2 2.5 fusion.54
  281.3 22.0 %collective-permute-done.25 = bf16[4,64,2304]{2,1,0:T(8,128)(2,1)S(1)} collective-permute-done((bf16[4,64,2304]{2,1,0:T(8,128)(2,1)S(1)}, bf16[4,64,2304]{2,1,0:T(8,128)(2,1)S(1)}, u32[]{:S(2)}, u32[]{:S(2)}) %collective-permute-start.25) | collective-permute-done | bytes 1179680 | tf_op jit(solution)/shard_map/ppermute | solution.py:24
  307.9 20.3 %shard_map.247 = (f32[2,4,256,64]{3,2,1,0:T(8,128)S(1)}, bf16[16,2,4,128,128]{4,3,2,1,0:T(8,128)(2,1)}) custom-call(bf16[2,4,256,64]{3,2,1,0:T(8,128)(2,1)S(1)} %bitcast.175, bf16[16,2,4,128,128]{4,3,2,1,0:T(8,128)(2,1)} %constant_dynamic-update-slice_fusion.9.pair_ref, s32[2,256,1]{2,1,0:T(8,128)S(1)} %tile.12.query_place_ref, s32[2,1,2048]{2,1,0:T(1,128)S(1)} %bitcast.179, ...), custom_call_target="tpu_custom_call" | custom-call | flops 3221225472 | bytes 8388608 | tf_op jit(solution)/shard_map/pallas_call | solution.py:194
  328.2 2.9 collective-permute-done.26
  331.1 3.1 slice.288
  342.0 9.1 %collective-permute-done.21 = bf16[256,1024]{0,1:T(8,128)(2,1)} collective-permute-done((bf16[256,1024]{0,1:T(8,128)(2,1)}, bf16[256,1024]{0,1:T(8,128)(2,1)}, u32[]{:S(2)}, u32[]{:S(2)}) %collective-permute-start.21) | collective-permute-done | bytes 524320 | tf_op jit(solution)/shard_map/ppermute | solution.py:24
  351.2 3.4 fusion.24
  354.5 2.4 fusion.1
  358.2 2.7 add_convert_fusion
  370.9 16.8 %collective-permute-done.28 = bf16[4,2,4,128,128]{4,3,2,1,0:T(8,128)(2,1)} collective-permute-done((bf16[4,2,4,128,128]{4,3,2,1,0:T(8,128)(2,1)}, bf16[4,2,4,128,128]{4,3,2,1,0:T(8,128)(2,1)}, u32[]{:S(2)}, u32[]{:S(2)}) %collective-permute-start.28) | collective-permute-done | bytes 1048608 | tf_op jit(solution)/shard_map/ppermute | solution.py:24
  397.4 2.5 multiply_convert_fusion.5
  400.0 3.1 collective-permute-done.29
  404.3 3.4 collective-permute-start.30
  411.1 13.2 %collective-permute-done.30 = bf16[1,2,4,128,128]{4,3,2,1,0:T(8,128)(2,1)S(1)} collective-permute-done((bf16[1,2,4,128,128]{4,3,2,1,0:T(8,128)(2,1)S(1)}, bf16[1,2,4,128,128]{4,3,2,1,0:T(8,128)(2,1)S(1)}, u32[]{:S(2)}, u32[]{:S(2)}) %collective-permute-start.30) | collective-permute-done | bytes 262176 | tf_op jit(solution)/shard_map/ppermute | solution.py:24
  427.5 7.9 %collective-permute-done.32 = bf16[4,64,2304]{2,1,0:T(8,128)(2,1)} collective-permute-done((bf16[4,64,2304]{2,1,0:T(8,128)(2,1)}, bf16[4,64,2304]{2,1,0:T(8,128)(2,1)}, u32[]{:S(2)}, u32[]{:S(2)}) %collective-permute-start.32) | collective-permute-done | bytes 1179680 | tf_op jit(solution)/shard_map/ppermute | solution.py:24
  435.5 2.3 convolution_convert_fusion.7
  447.2 6.0 %collective-permute-done.33 = bf16[272,1024]{1,0:T(8,128)(2,1)} collective-permute-done((bf16[272,1024]{1,0:T(8,128)(2,1)}, bf16[272,1024]{1,0:T(8,128)(2,1)}, u32[]{:S(2)}, u32[]{:S(2)}) %collective-permute-start.33) | collective-permute-done | bytes 557088 | tf_op jit(solution)/shard_map/ppermute | solution.py:24
  463.0 2.4 collective-permute-start.39
  467.3 11.4 %collective-permute-done.39 = bf16[1,64,2304]{2,1,0:T(8,128)(2,1)S(1)} collective-permute-done((bf16[1,64,2304]{2,1,0:T(8,128)(2,1)S(1)}, bf16[1,64,2304]{2,1,0:T(8,128)(2,1)S(1)}, u32[]{:S(2)}, u32[]{:S(2)}) %collective-permute-start.39) | collective-permute-done | bytes 294944 | tf_op jit(solution)/shard_map/ppermute | solution.py:24
  483.4 5.0 fusion.4
  488.4 15.5 %collective-permute-done.35 = bf16[4,80,1536]{2,1,0:T(8,128)(2,1)S(1)} collective-permute-done((bf16[4,80,1536]{2,1,0:T(8,128)(2,1)S(1)}, bf16[4,80,1536]{2,1,0:T(8,128)(2,1)S(1)}, u32[]{:S(2)}, u32[]{:S(2)}) %collective-permute-start.35) | collective-permute-done | bytes 983072 | tf_op jit(solution)/shard_map/ppermute | solution.py:24
  506.6 16.3 %collective-permute-done.36 = bf16[2,80,1536]{2,1,0:T(8,128)(2,1)S(1)} collective-permute-done((bf16[2,80,1536]{2,1,0:T(8,128)(2,1)S(1)}, bf16[2,80,1536]{2,1,0:T(8,128)(2,1)S(1)}, u32[]{:S(2)}, u32[]{:S(2)}) %collective-permute-start.36) | collective-permute-done | bytes 491552 | tf_op jit(solution)/shard_map/ppermute | solution.py:24
  524.0 10.9 %collective-permute-done.37 = bf16[1,80,1536]{2,1,0:T(8,128)(2,1)S(1)} collective-permute-done((bf16[1,80,1536]{2,1,0:T(8,128)(2,1)S(1)}, bf16[1,80,1536]{2,1,0:T(8,128)(2,1)S(1)}, u32[]{:S(2)}, u32[]{:S(2)}) %collective-permute-start.37) | collective-permute-done | bytes 245792 | tf_op jit(solution)/shard_map/ppermute | solution.py:24
  (407 shorter events, 151.5 us)
Async XLA Ops:
  0.6 34.9 %copy-start = (bf16[256,1024]{1,0:T(8,128)(2,1)S(1)}, bf16[256,1024]{1,0:T(8,128)(2,1)}, u32[]{:S(2)}) copy-start(bf16[256,1024]{1,0:T(8,128)(2,1)} %param.15) | copy-start | bytes 1572868
  0.7 34.8 %copy-start.54 = (bf16[512,64]{0,1:T(8,128)(2,1)S(1)}, bf16[512,64]{0,1:T(8,128)(2,1)}, u32[]{:S(2)}) copy-start(bf16[512,64]{0,1:T(8,128)(2,1)} %param.23) | copy-start | bytes 196612
  0.7 34.8 %copy-start.56 = (bf16[64,256]{1,0:T(8,128)(2,1)S(1)}, bf16[64,256]{1,0:T(8,128)(2,1)}, u32[]{:S(2)}) copy-start(bf16[64,256]{1,0:T(8,128)(2,1)} %param.20) | copy-start | bytes 98308
  5.2 15.3 %collective-permute-start = (bf16[1,80,1536]{2,1,0:T(8,128)(2,1)S(1)}, bf16[1,80,1536]{2,1,0:T(8,128)(2,1)S(1)}, u32[]{:S(2)}, u32[]{:S(2)}) collective-permute-start(bf16[1,80,1536]{2,1,0:T(8,128)(2,1)S(1)} %fusion.46), channel_id=1, source_target_pairs={{0,16},{2,18},{4,20},{6,22},{8,24},{10,26},{12,28},{14,30},{16,0},... | collective-permute-start | bytes 737288 | tf_op jit(solution)/shard_map/ppermute | solution.py:24
  20.5 12.5 %collective-permute-start.1 = (bf16[2,80,1536]{2,1,0:T(8,128)(2,1)S(1)}, bf16[2,80,1536]{2,1,0:T(8,128)(2,1)S(1)}, u32[]{:S(2)}, u32[]{:S(2)}) collective-permute-start(bf16[2,80,1536]{2,1,0:T(8,128)(2,1)S(1)} %pad_maximum_fusion.17), channel_id=1, source_target_pairs={{0,8},{2,10},{4,12},{6,14},{8,0},{10,2},{12,4},{14,6},{16,24},{18,... | collective-permute-start | bytes 1474568 | tf_op jit(solution)/shard_map/ppermute | solution.py:24
  34.1 22.2 %collective-permute-start.2 = (bf16[4,80,1536]{2,1,0:T(8,128)(2,1)}, bf16[4,80,1536]{2,1,0:T(8,128)(2,1)S(1)}, u32[]{:S(2)}, u32[]{:S(2)}) collective-permute-start(bf16[4,80,1536]{2,1,0:T(8,128)(2,1)} %pad_maximum_fusion.10), channel_id=1, source_target_pairs={{0,4},{2,6},{4,0},{6,2},{8,12},{10,14},{12,8},{14,10},{16,20},{18,... | collective-permute-start | bytes 2949128 | tf_op jit(solution)/shard_map/ppermute | solution.py:24
  36.5 20.1 %collective-permute-start.6 = (bf16[1,64,2304]{2,1,0:T(8,128)(2,1)S(1)}, bf16[1,64,2304]{2,1,0:T(8,128)(2,1)S(1)}, u32[]{:S(2)}, u32[]{:S(2)}) collective-permute-start(bf16[1,64,2304]{2,1,0:T(8,128)(2,1)S(1)} %bitcast.201), channel_id=1, source_target_pairs={{0,16},{2,18},{4,20},{6,22},{8,24},{10,26},{12,28},{14,30},{16,0},... | collective-permute-start | bytes 884744 | tf_op jit(solution)/shard_map/ppermute | solution.py:24
  56.5 19.2 %collective-permute-start.3 = (bf16[8,80,1536]{2,1,0:T(8,128)(2,1)S(1)}, bf16[8,80,1536]{2,1,0:T(8,128)(2,1)S(1)}, u32[]{:S(2)}, u32[]{:S(2)}) collective-permute-start(bf16[8,80,1536]{2,1,0:T(8,128)(2,1)S(1)} %pad_maximum_fusion.5), channel_id=1, source_target_pairs={{0,2},{2,0},{4,6},{6,4},{8,10},{10,8},{12,14},{14,12},{16,18},{18,... | collective-permute-start | bytes 5898248 | tf_op jit(solution)/shard_map/ppermute | solution.py:24
  56.7 16.3 %collective-permute-start.7 = (bf16[2,64,2304]{2,1,0:T(8,128)(2,1)S(1)}, bf16[2,64,2304]{2,1,0:T(8,128)(2,1)S(1)}, u32[]{:S(2)}, u32[]{:S(2)}) collective-permute-start(bf16[2,64,2304]{2,1,0:T(8,128)(2,1)S(1)} %pad_maximum_fusion.11), channel_id=1, source_target_pairs={{0,8},{2,10},{4,12},{6,14},{8,0},{10,2},{12,4},{14,6},{16,24},{18,... | collective-permute-start | bytes 1769480 | tf_op jit(solution)/shard_map/ppermute | solution.py:24
  74.1 47.8 %collective-permute-start.8 = (bf16[4,64,2304]{2,1,0:T(8,128)(2,1)}, bf16[4,64,2304]{2,1,0:T(8,128)(2,1)}, u32[]{:S(2)}, u32[]{:S(2)}) collective-permute-start(bf16[4,64,2304]{2,1,0:T(8,128)(2,1)} %pad_maximum_fusion.6), channel_id=1, source_target_pairs={{0,4},{2,6},{4,0},{6,2},{8,12},{10,14},{12,8},{14,10},{16,20},{18,... | collective-permute-start | bytes 3538952 | tf_op jit(solution)/shard_map/ppermute | solution.py:24
  77.7 46.6 %copy-start.11 = (bf16[16,64,1024]{2,1,0:T(8,128)(2,1)}, bf16[16,64,1024]{2,1,0:T(8,128)(2,1)S(1)}, u32[]{:S(2)}) copy-start(bf16[16,64,1024]{2,1,0:T(8,128)(2,1)S(1)} %slice.345) | copy-start | bytes 6291460
  96.8 22.6 %collective-permute-start.4 = (bf16[1,2,4,128,128]{4,3,2,1,0:T(8,128)(2,1)S(1)}, bf16[1,2,4,128,128]{4,3,2,1,0:T(8,128)(2,1)S(1)}, u32[]{:S(2)}, u32[]{:S(2)}) collective-permute-start(bf16[1,2,4,128,128]{4,3,2,1,0:T(8,128)(2,1)S(1)} %maximum_bitcast_fusion.2), channel_id=1, source_target_pairs={{0,16},{2,18},{4,20},{6,22},{8,24},{10,26},{12,28},{14,30},{16,0},... | collective-permute-start | bytes 786440 | tf_op jit(solution)/shard_map/ppermute | solution.py:24
  100.6 36.1 %collective-permute-start.13 = (bf16[1,64,2304]{2,1,0:T(8,128)(2,1)}, bf16[1,64,2304]{2,1,0:T(8,128)(2,1)S(1)}, u32[]{:S(2)}, u32[]{:S(2)}) collective-permute-start(bf16[1,64,2304]{2,1,0:T(8,128)(2,1)} %bitcast.204), channel_id=1, source_target_pairs={{0,16},{2,18},{4,20},{6,22},{8,24},{10,26},{12,28},{14,30},{16,0},... | collective-permute-start | bytes 884744 | tf_op jit(solution)/shard_map/ppermute | solution.py:24
  119.4 16.5 %collective-permute-start.5 = (bf16[2,2,4,128,128]{4,3,2,1,0:T(8,128)(2,1)S(1)}, bf16[2,2,4,128,128]{4,3,2,1,0:T(8,128)(2,1)S(1)}, u32[]{:S(2)}, u32[]{:S(2)}) collective-permute-start(bf16[2,2,4,128,128]{4,3,2,1,0:T(8,128)(2,1)S(1)} %pad_maximum_fusion.14), channel_id=1, source_target_pairs={{0,8},{2,10},{4,12},{6,14},{8,0},{10,2},{12,4},{14,6},{16,24},{18,... | collective-permute-start | bytes 1572872 | tf_op jit(solution)/shard_map/ppermute | solution.py:24
  136.1 25.3 %collective-permute-start.9 = (bf16[4,2,4,128,128]{4,3,2,1,0:T(8,128)(2,1)S(1)}, bf16[4,2,4,128,128]{4,3,2,1,0:T(8,128)(2,1)}, u32[]{:S(2)}, u32[]{:S(2)}) collective-permute-start(bf16[4,2,4,128,128]{4,3,2,1,0:T(8,128)(2,1)S(1)} %pad_maximum_fusion.9), channel_id=1, source_target_pairs={{0,4},{2,6},{4,0},{6,2},{8,12},{10,14},{12,8},{14,10},{16,20},{18,... | collective-permute-start | bytes 3145736 | tf_op jit(solution)/shard_map/ppermute | solution.py:24
  137.6 27.0 %collective-permute-start.14 = (bf16[2,64,2304]{2,1,0:T(8,128)(2,1)}, bf16[2,64,2304]{2,1,0:T(8,128)(2,1)}, u32[]{:S(2)}, u32[]{:S(2)}) collective-permute-start(bf16[2,64,2304]{2,1,0:T(8,128)(2,1)} %pad_maximum_fusion.12), channel_id=1, source_target_pairs={{0,8},{2,10},{4,12},{6,14},{8,0},{10,2},{12,4},{14,6},{16,24},{18,... | collective-permute-start | bytes 1769480 | tf_op jit(solution)/shard_map/ppermute | solution.py:24
  164.5 51.5 %collective-permute-start.10 = (bf16[8,2,4,128,128]{4,3,2,1,0:T(8,128)(2,1)}, bf16[8,2,4,128,128]{4,3,2,1,0:T(8,128)(2,1)}, u32[]{:S(2)}, u32[]{:S(2)}) collective-permute-start(bf16[8,2,4,128,128]{4,3,2,1,0:T(8,128)(2,1)} %get-tuple-element.80), channel_id=1, source_target_pairs={{0,2},{2,0},{4,6},{6,4},{8,10},{10,8},{12,14},{14,12},{16,18},{18,... | collective-permute-start | bytes 6291464 | tf_op jit(solution)/shard_map/ppermute | solution.py:24
  170.2 16.6 %collective-permute-start.17 = (bf16[1,64,2304]{2,1,0:T(8,128)(2,1)S(1)}, bf16[1,64,2304]{2,1,0:T(8,128)(2,1)S(1)}, u32[]{:S(2)}, u32[]{:S(2)}) collective-permute-start(bf16[1,64,2304]{2,1,0:T(8,128)(2,1)S(1)} %bitcast.207), channel_id=1, source_target_pairs={{0,16},{2,18},{4,20},{6,22},{8,24},{10,26},{12,28},{14,30},{16,0},... | collective-permute-start | bytes 884744 | tf_op jit(solution)/shard_map/ppermute | solution.py:24
  187.7 15.2 %collective-permute-start.18 = (bf16[2,64,2304]{2,1,0:T(8,128)(2,1)}, bf16[2,64,2304]{2,1,0:T(8,128)(2,1)}, u32[]{:S(2)}, u32[]{:S(2)}) collective-permute-start(bf16[2,64,2304]{2,1,0:T(8,128)(2,1)} %pad_maximum_fusion.13), channel_id=1, source_target_pairs={{0,8},{2,10},{4,12},{6,14},{8,0},{10,2},{12,4},{14,6},{16,24},{18,... | collective-permute-start | bytes 1769480 | tf_op jit(solution)/shard_map/ppermute | solution.py:24
  187.7 27.8 %collective-permute-start.15 = (bf16[4,64,2304]{2,1,0:T(8,128)(2,1)}, bf16[4,64,2304]{2,1,0:T(8,128)(2,1)}, u32[]{:S(2)}, u32[]{:S(2)}) collective-permute-start(bf16[4,64,2304]{2,1,0:T(8,128)(2,1)} %pad_maximum_fusion.7), channel_id=1, source_target_pairs={{0,4},{2,6},{4,0},{6,2},{8,12},{10,14},{12,8},{14,10},{16,20},{18,... | collective-permute-start | bytes 3538952 | tf_op jit(solution)/shard_map/ppermute | solution.py:24
  215.6 31.3 %collective-permute-start.19 = (bf16[4,64,2304]{2,1,0:T(8,128)(2,1)}, bf16[4,64,2304]{2,1,0:T(8,128)(2,1)}, u32[]{:S(2)}, u32[]{:S(2)}) collective-permute-start(bf16[4,64,2304]{2,1,0:T(8,128)(2,1)} %pad_maximum_fusion.8), channel_id=1, source_target_pairs={{0,4},{2,6},{4,0},{6,2},{8,12},{10,14},{12,8},{14,10},{16,20},{18,... | collective-permute-start | bytes 3538952 | tf_op jit(solution)/shard_map/ppermute | solution.py:24
  233.7 12.4 %collective-permute-start.11 = (bf16[256,1024]{0,1:T(8,128)(2,1)S(1)}, bf16[256,1024]{0,1:T(8,128)(2,1)S(1)}, u32[]{:S(2)}, u32[]{:S(2)}) collective-permute-start(bf16[256,1024]{0,1:T(8,128)(2,1)S(1)} %convolution_convert_fusion.5), channel_id=1, source_target_pairs={{0,1},{1,0},{2,3},{3,2},{4,5},{5,4},{6,7},{7,6},{8,9},{9,8},{10,11... | collective-permute-start | bytes 1572872 | tf_op jit(solution)/shard_map/ppermute | solution.py:24
  238.6 11.1 %collective-permute-start.16 = (bf16[8,64,2304]{2,1,0:T(8,128)(2,1)}, bf16[8,64,2304]{2,1,0:T(8,128)(2,1)}, u32[]{:S(2)}, u32[]{:S(2)}) collective-permute-start(bf16[8,64,2304]{2,1,0:T(8,128)(2,1)} %pad_maximum_fusion.3), channel_id=1, source_target_pairs={{0,2},{2,0},{4,6},{6,4},{8,10},{10,8},{12,14},{14,12},{16,18},{18,... | collective-permute-start | bytes 7077896 | tf_op jit(solution)/shard_map/ppermute | solution.py:24
  238.7 15.0 %collective-permute-start.12 = (bf16[8,64,2304]{2,1,0:T(8,128)(2,1)}, bf16[8,64,2304]{2,1,0:T(8,128)(2,1)S(1)}, u32[]{:S(2)}, u32[]{:S(2)}) collective-permute-start(bf16[8,64,2304]{2,1,0:T(8,128)(2,1)} %constant_dynamic-update-slice_fusion.5), channel_id=1, source_target_pairs={{0,2},{2,0},{4,6},{6,4},{8,10},{10,8},{12,14},{14,12},{16,18},{18,... | collective-permute-start | bytes 7077896 | tf_op jit(solution)/shard_map/ppermute | solution.py:24
  248.8 7.0 %collective-permute-start.20 = (bf16[8,64,2304]{2,1,0:T(8,128)(2,1)S(1)}, bf16[8,64,2304]{2,1,0:T(8,128)(2,1)S(1)}, u32[]{:S(2)}, u32[]{:S(2)}) collective-permute-start(bf16[8,64,2304]{2,1,0:T(8,128)(2,1)S(1)} %pad_maximum_fusion.4), channel_id=1, source_target_pairs={{0,2},{2,0},{4,6},{6,4},{8,10},{10,8},{12,14},{14,12},{16,18},{18,... | collective-permute-start | bytes 7077896 | tf_op jit(solution)/shard_map/ppermute | solution.py:24
  265.6 8.6 %collective-permute-start.22 = (bf16[8,64,2304]{2,1,0:T(8,128)(2,1)S(1)}, bf16[8,64,2304]{2,1,0:T(8,128)(2,1)S(1)}, u32[]{:S(2)}, u32[]{:S(2)}) collective-permute-start(bf16[8,64,2304]{2,1,0:T(8,128)(2,1)S(1)} %bitcast.195), channel_id=1, source_target_pairs={{0,2},{2,0},{4,6},{6,4},{8,10},{10,8},{12,14},{14,12},{16,18},{18,... | collective-permute-start | bytes 7077896 | tf_op jit(solution)/shard_map/ppermute | solution.py:24
  267.8 11.6 %collective-permute-start.24 = (bf16[8,64,2304]{2,1,0:T(8,128)(2,1)S(1)}, bf16[8,64,2304]{2,1,0:T(8,128)(2,1)S(1)}, u32[]{:S(2)}, u32[]{:S(2)}) collective-permute-start(bf16[8,64,2304]{2,1,0:T(8,128)(2,1)S(1)} %bitcast.194), channel_id=1, source_target_pairs={{0,2},{2,0},{4,6},{6,4},{8,10},{10,8},{12,14},{14,12},{16,18},{18,... | collective-permute-start | bytes 7077896 | tf_op jit(solution)/shard_map/ppermute | solution.py:24
  272.7 81.9 %collective-permute-start.31 = (bf16[8,64,2304]{2,1,0:T(8,128)(2,1)}, bf16[8,64,2304]{2,1,0:T(8,128)(2,1)}, u32[]{:S(2)}, u32[]{:S(2)}) collective-permute-start(bf16[8,64,2304]{2,1,0:T(8,128)(2,1)} %bitcast.49), channel_id=1, source_target_pairs={{0,2},{2,0},{4,6},{6,4},{8,10},{10,8},{12,14},{14,12},{16,18},{18,... | collective-permute-start | bytes 7077896 | tf_op jit(solution)/shard_map/ppermute | solution.py:24
  274.9 28.4 %collective-permute-start.25 = (bf16[4,64,2304]{2,1,0:T(8,128)(2,1)S(1)}, bf16[4,64,2304]{2,1,0:T(8,128)(2,1)S(1)}, u32[]{:S(2)}, u32[]{:S(2)}) collective-permute-start(bf16[4,64,2304]{2,1,0:T(8,128)(2,1)S(1)} %slice.360), channel_id=1, source_target_pairs={{0,4},{2,6},{4,0},{6,2},{8,12},{10,14},{12,8},{14,10},{16,20},{18,... | collective-permute-start | bytes 3538952 | tf_op jit(solution)/shard_map/ppermute | solution.py:24
  277.8 26.9 %collective-permute-start.23 = (bf16[256,1024]{0,1:T(8,128)(2,1)S(1)}, bf16[256,1024]{0,1:T(8,128)(2,1)S(1)}, u32[]{:S(2)}, u32[]{:S(2)}) collective-permute-start(bf16[256,1024]{0,1:T(8,128)(2,1)S(1)} %fusion.31), channel_id=1, source_target_pairs={{0,1},{1,0},{2,3},{3,2},{4,5},{5,4},{6,7},{7,6},{8,9},{9,8},{10,11... | collective-permute-start | bytes 1572872 | tf_op jit(solution)/shard_map/ppermute | solution.py:24
  303.3 27.9 %collective-permute-start.26 = (bf16[4,64,2304]{2,1,0:T(8,128)(2,1)}, bf16[4,64,2304]{2,1,0:T(8,128)(2,1)}, u32[]{:S(2)}, u32[]{:S(2)}) collective-permute-start(bf16[4,64,2304]{2,1,0:T(8,128)(2,1)} %slice.363), channel_id=1, source_target_pairs={{0,4},{2,6},{4,0},{6,2},{8,12},{10,14},{12,8},{14,10},{16,20},{18,... | collective-permute-start | bytes 3538952 | tf_op jit(solution)/shard_map/ppermute | solution.py:24
  334.3 23.9 %collective-permute-start.27 = (bf16[8,2,4,128,128]{4,3,2,1,0:T(8,128)(2,1)}, bf16[8,2,4,128,128]{4,3,2,1,0:T(8,128)(2,1)}, u32[]{:S(2)}, u32[]{:S(2)}) collective-permute-start(bf16[8,2,4,128,128]{4,3,2,1,0:T(8,128)(2,1)} %slice.288), channel_id=1, source_target_pairs={{0,2},{2,0},{4,6},{6,4},{8,10},{10,8},{12,14},{14,12},{16,18},{18,... | collective-permute-start | bytes 6291464 | tf_op jit(solution)/shard_map/ppermute | solution.py:24
  336.5 14.6 %collective-permute-start.21 = (bf16[256,1024]{0,1:T(8,128)(2,1)}, bf16[256,1024]{0,1:T(8,128)(2,1)}, u32[]{:S(2)}, u32[]{:S(2)}) collective-permute-start(bf16[256,1024]{0,1:T(8,128)(2,1)} %convolution_convert_fusion.6), channel_id=1, source_target_pairs={{0,1},{1,0},{2,3},{3,2},{4,5},{5,4},{6,7},{7,6},{8,9},{9,8},{10,11... | collective-permute-start | bytes 1572872 | tf_op jit(solution)/shard_map/ppermute | solution.py:24
  362.6 25.1 %collective-permute-start.28 = (bf16[4,2,4,128,128]{4,3,2,1,0:T(8,128)(2,1)}, bf16[4,2,4,128,128]{4,3,2,1,0:T(8,128)(2,1)}, u32[]{:S(2)}, u32[]{:S(2)}) collective-permute-start(bf16[4,2,4,128,128]{4,3,2,1,0:T(8,128)(2,1)} %slice.367), channel_id=1, source_target_pairs={{0,4},{2,6},{4,0},{6,2},{8,12},{10,14},{12,8},{14,10},{16,20},{18,... | collective-permute-start | bytes 3145736 | tf_op jit(solution)/shard_map/ppermute | solution.py:24
  369.3 38.3 %collective-permute-start.42 = (bf16[2,64,2304]{2,1,0:T(8,128)(2,1)}, bf16[2,64,2304]{2,1,0:T(8,128)(2,1)}, u32[]{:S(2)}, u32[]{:S(2)}) collective-permute-start(bf16[2,64,2304]{2,1,0:T(8,128)(2,1)} %slice.411), channel_id=1, source_target_pairs={{0,8},{2,10},{4,12},{6,14},{8,0},{10,2},{12,4},{14,6},{16,24},{18,... | collective-permute-start | bytes 1769480 | tf_op jit(solution)/shard_map/ppermute | solution.py:24
  390.1 13.0 %collective-permute-start.29 = (bf16[2,2,4,128,128]{4,3,2,1,0:T(8,128)(2,1)}, bf16[2,2,4,128,128]{4,3,2,1,0:T(8,128)(2,1)}, u32[]{:S(2)}, u32[]{:S(2)}) collective-permute-start(bf16[2,2,4,128,128]{4,3,2,1,0:T(8,128)(2,1)} %slice.369), channel_id=1, source_target_pairs={{0,8},{2,10},{4,12},{6,14},{8,0},{10,2},{12,4},{14,6},{16,24},{18,... | collective-permute-start | bytes 1572872 | tf_op jit(solution)/shard_map/ppermute | solution.py:24
  404.3 20.1 %collective-permute-start.30 = (bf16[1,2,4,128,128]{4,3,2,1,0:T(8,128)(2,1)S(1)}, bf16[1,2,4,128,128]{4,3,2,1,0:T(8,128)(2,1)S(1)}, u32[]{:S(2)}, u32[]{:S(2)}) collective-permute-start(bf16[1,2,4,128,128]{4,3,2,1,0:T(8,128)(2,1)S(1)} %slice.371), channel_id=1, source_target_pairs={{0,16},{2,18},{4,20},{6,22},{8,24},{10,26},{12,28},{14,30},{16,0},... | collective-permute-start | bytes 786440 | tf_op jit(solution)/shard_map/ppermute | solution.py:24
  409.6 55.8 %collective-permute-start.43 = (bf16[1,64,2304]{2,1,0:T(8,128)(2,1)}, bf16[1,64,2304]{2,1,0:T(8,128)(2,1)}, u32[]{:S(2)}, u32[]{:S(2)}) collective-permute-start(bf16[1,64,2304]{2,1,0:T(8,128)(2,1)} %slice.413), channel_id=1, source_target_pairs={{0,16},{2,18},{4,20},{6,22},{8,24},{10,26},{12,28},{14,30},{16,0},... | collective-permute-start | bytes 884744 | tf_op jit(solution)/shard_map/ppermute | solution.py:24
  409.7 25.8 %collective-permute-start.32 = (bf16[4,64,2304]{2,1,0:T(8,128)(2,1)}, bf16[4,64,2304]{2,1,0:T(8,128)(2,1)}, u32[]{:S(2)}, u32[]{:S(2)}) collective-permute-start(bf16[4,64,2304]{2,1,0:T(8,128)(2,1)} %slice.378), channel_id=1, source_target_pairs={{0,4},{2,6},{4,0},{6,2},{8,12},{10,14},{12,8},{14,10},{16,20},{18,... | collective-permute-start | bytes 3538952 | tf_op jit(solution)/shard_map/ppermute | solution.py:24
  441.7 11.5 %collective-permute-start.33 = (bf16[272,1024]{1,0:T(8,128)(2,1)}, bf16[272,1024]{1,0:T(8,128)(2,1)}, u32[]{:S(2)}, u32[]{:S(2)}) collective-permute-start(bf16[272,1024]{1,0:T(8,128)(2,1)} %copy.239), channel_id=1, source_target_pairs={{0,1},{1,0},{2,3},{3,2},{4,5},{5,4},{6,7},{7,6},{8,9},{9,8},{10,11... | collective-permute-start | bytes 1671176 | tf_op jit(solution)/shard_map/ppermute | solution.py:24
  445.7 15.0 %collective-permute-start.38 = (bf16[2,64,2304]{2,1,0:T(8,128)(2,1)}, bf16[2,64,2304]{2,1,0:T(8,128)(2,1)}, u32[]{:S(2)}, u32[]{:S(2)}) collective-permute-start(bf16[2,64,2304]{2,1,0:T(8,128)(2,1)} %slice.401), channel_id=1, source_target_pairs={{0,8},{2,10},{4,12},{6,14},{8,0},{10,2},{12,4},{14,6},{16,24},{18,... | collective-permute-start | bytes 1769480 | tf_op jit(solution)/shard_map/ppermute | solution.py:24
  460.6 18.9 %collective-permute-start.34 = (bf16[8,80,1536]{2,1,0:T(8,128)(2,1)S(1)}, bf16[8,80,1536]{2,1,0:T(8,128)(2,1)S(1)}, u32[]{:S(2)}, u32[]{:S(2)}) collective-permute-start(bf16[8,80,1536]{2,1,0:T(8,128)(2,1)S(1)} %slice.384), channel_id=1, source_target_pairs={{0,2},{2,0},{4,6},{6,4},{8,10},{10,8},{12,14},{14,12},{16,18},{18,... | collective-permute-start | bytes 5898248 | tf_op jit(solution)/shard_map/ppermute | solution.py:24
  463.0 15.7 %collective-permute-start.39 = (bf16[1,64,2304]{2,1,0:T(8,128)(2,1)S(1)}, bf16[1,64,2304]{2,1,0:T(8,128)(2,1)S(1)}, u32[]{:S(2)}, u32[]{:S(2)}) collective-permute-start(bf16[1,64,2304]{2,1,0:T(8,128)(2,1)S(1)} %slice.403), channel_id=1, source_target_pairs={{0,16},{2,18},{4,20},{6,22},{8,24},{10,26},{12,28},{14,30},{16,0},... | collective-permute-start | bytes 884744 | tf_op jit(solution)/shard_map/ppermute | solution.py:24
  480.2 23.7 %collective-permute-start.35 = (bf16[4,80,1536]{2,1,0:T(8,128)(2,1)S(1)}, bf16[4,80,1536]{2,1,0:T(8,128)(2,1)S(1)}, u32[]{:S(2)}, u32[]{:S(2)}) collective-permute-start(bf16[4,80,1536]{2,1,0:T(8,128)(2,1)S(1)} %slice.386), channel_id=1, source_target_pairs={{0,4},{2,6},{4,0},{6,2},{8,12},{10,14},{12,8},{14,10},{16,20},{18,... | collective-permute-start | bytes 2949128 | tf_op jit(solution)/shard_map/ppermute | solution.py:24
  483.3 21.0 %collective-permute-start.40 = (bf16[2,64,2304]{2,1,0:T(8,128)(2,1)S(1)}, bf16[2,64,2304]{2,1,0:T(8,128)(2,1)S(1)}, u32[]{:S(2)}, u32[]{:S(2)}) collective-permute-start(bf16[2,64,2304]{2,1,0:T(8,128)(2,1)S(1)} %slice.406), channel_id=1, source_target_pairs={{0,8},{2,10},{4,12},{6,14},{8,0},{10,2},{12,4},{14,6},{16,24},{18,... | collective-permute-start | bytes 1769480 | tf_op jit(solution)/shard_map/ppermute | solution.py:24
  504.2 18.7 %collective-permute-start.36 = (bf16[2,80,1536]{2,1,0:T(8,128)(2,1)S(1)}, bf16[2,80,1536]{2,1,0:T(8,128)(2,1)S(1)}, u32[]{:S(2)}, u32[]{:S(2)}) collective-permute-start(bf16[2,80,1536]{2,1,0:T(8,128)(2,1)S(1)} %slice.388), channel_id=1, source_target_pairs={{0,8},{2,10},{4,12},{6,14},{8,0},{10,2},{12,4},{14,6},{16,24},{18,... | collective-permute-start | bytes 1474568 | tf_op jit(solution)/shard_map/ppermute | solution.py:24
  504.5 18.6 %collective-permute-start.41 = (bf16[1,64,2304]{2,1,0:T(8,128)(2,1)S(1)}, bf16[1,64,2304]{2,1,0:T(8,128)(2,1)S(1)}, u32[]{:S(2)}, u32[]{:S(2)}) collective-permute-start(bf16[1,64,2304]{2,1,0:T(8,128)(2,1)S(1)} %slice.408), channel_id=1, source_target_pairs={{0,16},{2,18},{4,20},{6,22},{8,24},{10,26},{12,28},{14,30},{16,0},... | collective-permute-start | bytes 884744 | tf_op jit(solution)/shard_map/ppermute | solution.py:24
  523.0 11.8 %collective-permute-start.37 = (bf16[1,80,1536]{2,1,0:T(8,128)(2,1)S(1)}, bf16[1,80,1536]{2,1,0:T(8,128)(2,1)S(1)}, u32[]{:S(2)}, u32[]{:S(2)}) collective-permute-start(bf16[1,80,1536]{2,1,0:T(8,128)(2,1)S(1)} %slice.390), channel_id=1, source_target_pairs={{0,16},{2,18},{4,20},{6,22},{8,24},{10,26},{12,28},{14,30},{16,0},... | collective-permute-start | bytes 737288 | tf_op jit(solution)/shard_map/ppermute | solution.py:24
  (68 other events, 665.7 us)
